TPU v7x, 128 devices: a whole 4x4x4 slice. The times are simulated.
128 devices in a mesh: tile: 32 (over z, x, y_lo), lev: 4 (over y_hi, core).
Axes of the slice: x: 4, y: 4 (y_hi: 2, y_lo: 2; y = y_hi * 2 + y_lo), z: 4, core: 2. Of those that a mesh axis runs over, the one named last changes fastest.
Arguments:
- ensemble: bfloat16 [80, 4194304], P(None, ('tile', 'lev')), may hold values from -6 to 6
- obs_pert: bfloat16 [80, 2097152], P(None, ('tile', 'lev')), may hold values from -4 to 4
- innovation: float32 [2097152], P(('tile', 'lev')), may hold values from -12 to 12
- obs_rinv: float32 [2097152], P(('tile', 'lev')), may hold values from 0.25 to 4
- loc_weight: float32 [3, 2097152], P(None, ('tile', 'lev')), may hold values from 0.05 to 1
- obs_count: int32 [128], P(('tile', 'lev')), may hold values from 4096 to 16384, as said below
Outputs:
- analysis: bfloat16 [80, 4194304], P(None, ('tile', 'lev'))
Inputs may be any that keep to these rules, and one draw needn't show every extreme that they name: `obs_count`: some block has all 16384 slots valid in every draw.
All inputs are finite; a program needn't handle non-finite values.
Results may differ from a plain program's by a relative error of at most 0.007.
Values may be sent and summed in bfloat16 or wider, within the bound.
No kernel may reach another device: no remote copies, remote signals or barrier semaphores. Data moves between devices by JAX's collectives and lax.ppermute only.
A program may use at most 64 MiB of HBM per device.

v0:
```python
import jax
import jax.numpy as jnp
from jax import lax
from jax.sharding import PartitionSpec as P

NS_STEPS = 10


def extended(array, sides, width):
    for axis, dim in sides:
        devices, length = (lax.axis_size(axis), array.shape[dim])
        up = [(i, (i + 1) % devices) for i in range(devices)]
        down = [(j, i) for i, j in up]
        last = lax.slice_in_dim(array, length - width, length, axis=dim)
        initial = lax.slice_in_dim(array, 0, width, axis=dim)
        before = lax.ppermute(last, axis, up)
        after = lax.ppermute(initial, axis, down)
        array = jnp.concatenate([before, array, after], axis=dim)
    return array


def weighted_gram(pert, innov, weight):
    root = jnp.sqrt(weight)
    ext = (
        jnp.concatenate([pert.astype(jnp.float32), innov[None, :]], axis=0) * root[None, :]
    ).astype(jnp.bfloat16)
    return jnp.dot(ext, ext.T, preferred_element_type=jnp.float32)


def analyse(gram, ensemble):
    members = ensemble.shape[0]
    cov = gram[:members, :members]
    proj = gram[:members, members]
    eye = jnp.eye(members, dtype=jnp.float32)
    mat = (members - 1.0) * eye + cov
    scale = jnp.sqrt(jnp.sum(mat * mat))
    iterate = mat / scale
    inverse_root = eye
    for step in range(NS_STEPS):
        factor = 1.5 * eye - 0.5 * jnp.dot(inverse_root, iterate, precision=lax.Precision.HIGHEST)
        iterate = jnp.dot(iterate, factor, precision=lax.Precision.HIGHEST)
        inverse_root = jnp.dot(factor, inverse_root, precision=lax.Precision.HIGHEST)
    root_inv = inverse_root / jnp.sqrt(scale)
    precision_mat = jnp.dot(root_inv, root_inv, precision=lax.Precision.HIGHEST)
    mean_weight = jnp.dot(precision_mat, proj, precision=lax.Precision.HIGHEST)
    transform = (jnp.sqrt(members - 1.0) * root_inv + mean_weight[:, None]).astype(jnp.bfloat16)
    mean_state = jnp.mean(ensemble.astype(jnp.float32), axis=0)
    keep = 1.0 - jnp.sum(transform.astype(jnp.float32), axis=0)
    result = (
        jnp.dot(transform.T, ensemble, preferred_element_type=jnp.float32)
        + keep[:, None] * mean_state[None, :]
    )
    return result.astype(jnp.bfloat16)


def local(ensemble, obs_pert, innovation, obs_rinv, loc_weight, obs_count):
    width = obs_pert.shape[1]
    live = (lax.iota(jnp.int32, width) < obs_count[0]).astype(jnp.float32)
    side = jnp.stack(
        [
            innovation,
            obs_rinv * loc_weight[0] * live,
            obs_rinv * loc_weight[1] * live,
            obs_rinv * loc_weight[2] * live,
        ]
    ).astype(jnp.bfloat16)
    near_pert, near_side = (
        extended(obs_pert, (("tile", 1),), width),
        extended(side, (("tile", 1),), width),
    )
    near32 = near_side.astype(jnp.float32)
    total = jnp.zeros((obs_pert.shape[0] + 1, obs_pert.shape[0] + 1), jnp.float32)
    for segment, row in ((0, 3), (1, 2), (2, 1)):
        lower = segment * width
        total = total + weighted_gram(
            near_pert[:, lower : lower + width],
            near32[0, lower : lower + width],
            near32[row, lower : lower + width],
        )
    total = lax.psum(total, "lev")
    return analyse(total, ensemble)


def solution(mesh):
    return jax.shard_map(
        local,
        mesh=mesh,
        in_specs=(
            P(None, ("tile", "lev")),
            P(None, ("tile", "lev")),
            P(("tile", "lev")),
            P(("tile", "lev")),
            P(None, ("tile", "lev")),
            P(("tile", "lev")),
        ),
        out_specs=P(None, ("tile", "lev")),
        check_vma=False,
    )
```

profile of v0, /device:TPU:1, one launch (start us, length us, event | category | flops | bytes accessed | tf_op | source)
XLA Modules:
  0.0 157.5 jit_solution(5623658565135964067)
XLA Ops:
  0.0 0.0 copy-start
  0.0 1.4 fusion.44
  2.1 0.9 select_convert_fusion.2
  3.1 0.8 convert.16
  4.0 0.3 pad_maximum_fusion
  4.3 2.2 %collective-permute-start.1 = (bf16[4,16384]{1,0:T(4,128)(2,1)S(1)}, bf16[4,16384]{1,0:T(4,128)(2,1)S(1)}, u32[]{:S(2)}, u32[]{:S(2)}) collective-permute-start(bf16[4,16384]{1,0:T(4,128)(2,1)S(1)} %pad_maximum_fusion), channel_id=1, source_target_pairs={{0,4},{4,8},{8,12},{12,16},{16,20},{20,24},{24,28},{28,32},{32,36}... | collective-permute-start | bytes 393224 | tf_op jit(solution)/shard_map/ppermute | solution.py:16
  6.5 5.8 %collective-permute-start.2 = (bf16[4,16384]{1,0:T(4,128)(2,1)S(1)}, bf16[4,16384]{1,0:T(4,128)(2,1)S(1)}, u32[]{:S(2)}, u32[]{:S(2)}) collective-permute-start(bf16[4,16384]{1,0:T(4,128)(2,1)S(1)} %pad_maximum_fusion), channel_id=1, source_target_pairs={{4,0},{8,4},{12,8},{16,12},{20,16},{24,20},{28,24},{32,28},{36,32}... | collective-permute-start | bytes 393224 | tf_op jit(solution)/shard_map/ppermute | solution.py:17
  12.3 1.4 collective-permute-start.3
  13.6 0.1 collective-permute-start
  13.7 3.4 %convert_reduce_fusion = f32[32768]{0:T(1024)S(1)} fusion(bf16[80,32768]{1,0:T(8,128)(2,1)} %param.6), kind=kLoop, calls=%fused_computation.2 | loop fusion | flops 5210112 | bytes 5373952 | tf_op jit(solution)/shard_map/reduce_sum | solution.py:47
  17.1 0.0 copy-done
  17.2 0.4 convert_element_type.39
  17.6 0.0 collective-permute-done.1
  17.6 0.0 collective-permute-done.2
  17.6 0.8 convert_sqrt_fusion.1
  18.4 0.4 maximum_convert_fusion.2
  18.8 1.0 fusion.6
  19.8 106.6 %collective-permute-done.3 = bf16[80,16384]{1,0:T(8,128)(2,1)S(1)} collective-permute-done((bf16[80,16384]{1,0:T(8,128)(2,1)}, bf16[80,16384]{1,0:T(8,128)(2,1)S(1)}, u32[]{:S(2)}, u32[]{:S(2)}) %collective-permute-start.3) | collective-permute-done | bytes 2621472 | tf_op jit(solution)/shard_map/ppermute | solution.py:17
  126.4 0.4 convert_element_type.41
  126.9 1.0 fusion.4
  127.9 0.0 collective-permute-done
  127.9 0.4 convert_element_type.36
  128.3 1.0 fusion.26
  129.3 14.5 %psum.7 = f32[81,81]{1,0:T(8,128)S(1)} all-reduce(f32[81,81]{1,0:T(8,128)S(1)} %fusion.26), channel_id=1, replica_groups=mesh['tile'=32,'lev'=4] {'lev'}, use_global_device_ids=true, to_apply=%region_0.0 | all-reduce | flops 6561 | bytes 52488 | tf_op jit(solution)/shard_map/psum | solution.py:80
  143.9 0.6 multiply_reduce_fusion
  145.2 0.2 fusion.22
  145.3 0.2 fusion.33
  145.5 0.1 fusion.31
  145.7 0.2 fusion.21
  145.9 0.2 fusion.46
  146.0 0.2 fusion.45
  146.2 0.2 fusion.20
  146.4 0.2 fusion.48
  146.6 0.2 fusion.47
  146.8 0.2 fusion.19
  146.9 0.2 fusion.50
  147.1 0.2 fusion.49
  147.3 0.2 fusion.18
  147.5 0.2 fusion.52
  147.7 0.2 fusion.51
  147.8 0.2 fusion.17
  148.0 0.2 fusion.54
  148.2 0.2 fusion.53
  148.4 0.2 fusion.16
  148.5 0.2 fusion.56
  148.7 0.2 fusion.55
  148.9 0.2 fusion.15
  149.1 0.2 fusion.58
  149.3 0.2 fusion.57
  149.4 0.2 fusion.14
  149.6 0.2 fusion.60
  149.8 0.2 fusion.59
  150.0 0.2 slice_reduce_fusion
  150.2 0.2 fusion.13
  150.4 0.2 convolution_divide_fusion
  150.6 0.2 fusion.61
  150.7 0.2 convolution_bitcast_fusion
  150.9 0.1 convert_reduce_fusion.1
  151.0 6.5 %fusion = bf16[80,32768]{1,0:T(8,128)(2,1)} fusion(bf16[80,32768]{1,0:T(8,128)(2,1)} %param.6, f32[32768]{0:T(1024)S(1)} %broadcast_multiply_fusion, f32[80]{0:T(128)S(1)} %broadcast_subtract_fusion, f32[80,80]{1,0:T(8,128)S(1)} %convolution_divide_fusion, f32[80]{0:T(128)S(1)} %convolution_bitcast_fusion), kind=kOutput, calls=%fused_computation.1 | convolution fusion | flops 427313920 | bytes 10643072 | tf_op jit(solution)/shard_map/dot_general | solution.py:50
  (6 shorter events, 0.2 us)
Async XLA Ops:
  0.0 17.1 %copy-start = (bf16[80,16384]{1,0:T(8,128)(2,1)S(1)}, bf16[80,16384]{1,0:T(8,128)(2,1)}, u32[]{:S(2)}) copy-start(bf16[80,16384]{1,0:T(8,128)(2,1)} %param.7) | copy-start | bytes 7864324
  4.3 13.3 %collective-permute-start.1 = (bf16[4,16384]{1,0:T(4,128)(2,1)S(1)}, bf16[4,16384]{1,0:T(4,128)(2,1)S(1)}, u32[]{:S(2)}, u32[]{:S(2)}) collective-permute-start(bf16[4,16384]{1,0:T(4,128)(2,1)S(1)} %pad_maximum_fusion), channel_id=1, source_target_pairs={{0,4},{4,8},{8,12},{12,16},{16,20},{20,24},{24,28},{28,32},{32,36}... | collective-permute-start | bytes 393224 | tf_op jit(solution)/shard_map/ppermute | solution.py:16
  6.5 11.1 %collective-permute-start.2 = (bf16[4,16384]{1,0:T(4,128)(2,1)S(1)}, bf16[4,16384]{1,0:T(4,128)(2,1)S(1)}, u32[]{:S(2)}, u32[]{:S(2)}) collective-permute-start(bf16[4,16384]{1,0:T(4,128)(2,1)S(1)} %pad_maximum_fusion), channel_id=1, source_target_pairs={{4,0},{8,4},{12,8},{16,12},{20,16},{24,20},{28,24},{32,28},{36,32}... | collective-permute-start | bytes 393224 | tf_op jit(solution)/shard_map/ppermute | solution.py:17
  12.3 114.2 %collective-permute-start.3 = (bf16[80,16384]{1,0:T(8,128)(2,1)}, bf16[80,16384]{1,0:T(8,128)(2,1)S(1)}, u32[]{:S(2)}, u32[]{:S(2)}) collective-permute-start(bf16[80,16384]{1,0:T(8,128)(2,1)} %param.7), channel_id=1, source_target_pairs={{4,0},{8,4},{12,8},{16,12},{20,16},{24,20},{28,24},{32,28},{36,32}... | collective-permute-start | bytes 7864328 | tf_op jit(solution)/shard_map/ppermute | solution.py:17
  13.6 114.2 %collective-permute-start = (bf16[80,16384]{1,0:T(8,128)(2,1)}, bf16[80,16384]{1,0:T(8,128)(2,1)S(1)}, u32[]{:S(2)}, u32[]{:S(2)}) collective-permute-start(bf16[80,16384]{1,0:T(8,128)(2,1)} %param.7), channel_id=1, source_target_pairs={{0,4},{4,8},{8,12},{12,16},{16,20},{20,24},{24,28},{28,32},{32,36}... | collective-permute-start | bytes 7864328 | tf_op jit(solution)/shard_map/ppermute | solution.py:16
where the time goes:
time: 159 us; the launch traced here: 158 us
  waiting for transfers between devices  107 us (67%)
  matrix products  14.8 us (9%)
  blocking collectives  14.5 us (9%)
  starting transfers between devices  9.41 us (6%)
  other arithmetic  8.61 us (5%)
  between operations  1.78 us (1%)
  local copies, waits for them, and re-layouts  1.77 us (1%)
    ppermute x2, waiting for transfers between devices, extended(): after = lax.ppermute(initial, axis, down)  107 us
    psum x1, blocking collectives, local(): total = lax.psum(total, 'lev')  14.5 us
    ppermute x2, starting transfers between devices, extended(): after = lax.ppermute(initial, axis, down)  7.13 us
    dot_general x1, matrix products, analyse(): jnp.dot(transform.T, ensemble, preferred_element_type=jnp.float32)  6.47 us
    reduce_sum x1, other arithmetic, analyse(): mean_state = jnp.mean(ensemble.astype(jnp.float32), axis=0)  3.39 us
  transfers between devices with their start and end apart: 4, of which 1 were waited for; matrix products, arithmetic and copies ran while one was open for 5% of the time, Pallas kernels for 0%

commit v1 on v0

v1 whole, which is shorter than its diff:
```python
import functools
import math

import jax
import jax.numpy as jnp
from jax import lax
from jax.experimental import pallas as pl
from jax.experimental.pallas import tpu as pltpu
from jax.sharding import PartitionSpec as P

NS_STEPS = 10
GRAM_CHUNKS = 4
COPY_CHUNKS = 8
PIECE = 1024
VMEM_BYTES = 40 * 1024 * 1024


def gram_kernel(info, pert, innov, rinv, loc, out):
    step = pl.program_id(0)
    members, width = pert.shape
    slots = step * width + lax.broadcasted_iota(jnp.int32, (1, width), 1)
    live = (slots < info[0]).astype(jnp.float32)
    even = info[1] == 0
    scaled = rinv[...]
    before, own, after = [
        (scaled * loc[i : i + 1, :] * live).astype(jnp.bfloat16) for i in range(3)
    ]
    near = jnp.where(even, after, before)
    far = jnp.where(even, before, after)
    block = pert[...]
    right = jnp.concatenate(
        [block, jnp.broadcast_to(innov[...].astype(jnp.bfloat16), (16, width))], axis=0
    )
    left = jnp.concatenate([block * far, block * near, block * own], axis=0)
    gram = lax.dot_general(left, right, (((1,), (1,)), ((), ())), preferred_element_type=jnp.float32)

    @pl.when(step == 0)
    def _():
        out[...] = jnp.zeros_like(out)

    out[:, : members + 16] += gram


def grams(pert, innov, rinv, loc, info):
    members, width = pert.shape
    chunk = width // GRAM_CHUNKS
    return pl.pallas_call(
        gram_kernel,
        grid=(GRAM_CHUNKS,),
        in_specs=[
            pl.BlockSpec(memory_space=pltpu.SMEM),
            pl.BlockSpec((members, chunk), lambda i: (0, i)),
            pl.BlockSpec((1, chunk), lambda i: (0, i)),
            pl.BlockSpec((1, chunk), lambda i: (0, i)),
            pl.BlockSpec((3, chunk), lambda i: (0, i)),
        ],
        out_specs=pl.BlockSpec((3 * members, 128), lambda i: (0, 0)),
        out_shape=jax.ShapeDtypeStruct((3 * members, 128), jnp.float32),
        compiler_params=pltpu.CompilerParams(vmem_limit_bytes=VMEM_BYTES),
        name="grams",
    )(info, pert, innov, rinv, loc)


def exact(a, b):
    return jnp.dot(a, b, precision=lax.Precision.HIGHEST, preferred_element_type=jnp.float32)


def transform_of(total):
    members = total.shape[0]
    rows = lax.broadcasted_iota(jnp.int32, total.shape, 0)
    cols = lax.broadcasted_iota(jnp.int32, total.shape, 1)
    eye = (rows == cols).astype(jnp.float32)[:, :members]
    mat = (members - 1.0) * eye + total[:, :members]
    scale = jnp.sqrt(jnp.sum(mat * mat))
    iterate = mat / scale
    factor = 1.5 * eye - 0.5 * iterate
    inverse_root = factor
    iterate = exact(iterate, factor)
    for _ in range(NS_STEPS - 1):
        factor = 1.5 * eye - 0.5 * exact(inverse_root, iterate)
        iterate = exact(iterate, factor)
        inverse_root = exact(factor, inverse_root)
    root_inv = inverse_root / jnp.sqrt(scale)
    mean_weight = exact(root_inv, exact(root_inv, total))[:, members : members + 1]
    transform = (math.sqrt(members - 1.0) * root_inv + mean_weight).astype(jnp.bfloat16)
    flipped = transform.astype(jnp.float32).T
    keep = 1.0 - jnp.sum(flipped, axis=1, keepdims=True)
    return flipped + keep / members


def analysis_kernel(own, other, mine, theirs, ensemble, out, held, result, left, in_sem, out_sem):
    members, width = held.shape
    chunk = width // COPY_CHUNKS

    def fetch(i):
        part = pl.ds(i * chunk, chunk)
        return pltpu.make_async_copy(ensemble.at[:, part], held.at[:, part], in_sem.at[i])

    def store(i):
        part = pl.ds(i * chunk, chunk)
        return pltpu.make_async_copy(result.at[:, part], out.at[:, part], out_sem.at[i])

    for i in range(COPY_CHUNKS):
        fetch(i).start()
    weights = transform_of(own[...] + other[...] + mine[...] + theirs[...])
    high = weights.astype(jnp.bfloat16)
    low = (weights - high.astype(jnp.float32)).astype(jnp.bfloat16)
    left[...] = jnp.concatenate([high, low], axis=1)

    for i in range(COPY_CHUNKS):
        fetch(i).wait()

        @pl.loop(0, chunk // PIECE)
        def _(j):
            part = pl.ds(pl.multiple_of(i * chunk + j * PIECE, PIECE), PIECE)
            block = held[:, part]
            both = jnp.concatenate([block, block], axis=0)
            result[:, part] = jnp.dot(
                left[...], both, preferred_element_type=jnp.float32
            ).astype(jnp.bfloat16)

        store(i).start()
    for i in range(COPY_CHUNKS):
        store(i).wait()


def analysis(own, other, mine, theirs, ensemble):
    members, width = ensemble.shape
    small = pl.BlockSpec(memory_space=pltpu.VMEM)
    return pl.pallas_call(
        analysis_kernel,
        in_specs=[small] * 4 + [pl.BlockSpec(memory_space=pl.ANY)],
        out_specs=pl.BlockSpec(memory_space=pl.ANY),
        out_shape=jax.ShapeDtypeStruct((members, width), jnp.bfloat16),
        scratch_shapes=[
            pltpu.VMEM((members, width), jnp.bfloat16),
            pltpu.VMEM((members, width), jnp.bfloat16),
            pltpu.VMEM((members, 2 * members), jnp.bfloat16),
            pltpu.SemaphoreType.DMA((COPY_CHUNKS,)),
            pltpu.SemaphoreType.DMA((COPY_CHUNKS,)),
        ],
        compiler_params=pltpu.CompilerParams(vmem_limit_bytes=VMEM_BYTES),
        name="analysis",
    )(own, other, mine, theirs, ensemble)


def local(n_tile, n_lev, ensemble, obs_pert, innovation, obs_rinv, loc_weight, obs_count):
    members = obs_pert.shape[0]
    axes = ("tile", "lev")

    def pairs(partner):
        return [
            (t * n_lev + l, (lambda a, b: a * n_lev + b)(*partner(t, l)))
            for t in range(n_tile)
            for l in range(n_lev)
        ]

    core = pairs(lambda t, l: (t, l ^ 1))
    high = pairs(lambda t, l: (t, l ^ 2))
    near = pairs(lambda t, l: (t ^ 1, l ^ (2 * (l & 1))))
    far = pairs(lambda t, l: ((t + 1 if t & 1 else t - 1) % n_tile, l ^ (2 * (l & 1))))

    parity = lax.rem(lax.axis_index("tile"), 2).astype(jnp.int32)
    info = jnp.concatenate([obs_count, parity[None]])
    gram = grams(obs_pert, innovation[None, :], obs_rinv[None, :], loc_weight, info)
    gram = gram + lax.ppermute(gram, axes, core)
    to_far, to_near, own = gram[:members], gram[members : 2 * members], gram[2 * members :]
    from_far = lax.ppermute(to_far, axes, far)
    from_near = lax.ppermute(to_near, axes, near)
    other = lax.ppermute(own, axes, high)
    mine = from_far + from_near
    theirs = lax.ppermute(mine, axes, core)
    return analysis(own, other, mine, theirs, ensemble)


def solution(mesh):
    return jax.shard_map(
        functools.partial(local, mesh.shape["tile"], mesh.shape["lev"]),
        mesh=mesh,
        in_specs=(
            P(None, ("tile", "lev")),
            P(None, ("tile", "lev")),
            P(("tile", "lev")),
            P(("tile", "lev")),
            P(None, ("tile", "lev")),
            P(("tile", "lev")),
        ),
        out_specs=P(None, ("tile", "lev")),
        check_vma=False,
    )
```

time: 159 us -> 39.7 us (0.25)
  waiting for transfers between devices: 107 us -> 4.47 us
  Pallas kernels: 0 us -> 15.5 us
  matrix products: 14.8 us -> 0 us
  blocking collectives: 14.5 us -> 0 us
  other arithmetic: 8.61 us -> 0.1 us
  local copies, waits for them, and re-layouts: 1.77 us -> 6.87 us
  starting transfers between devices: 9.41 us -> 11.7 us
    ppermute x4 -> x5, waiting for transfers between devices: 107 us -> 4.47 us  [the longest x1 2.17 us: local(): other = lax.ppermute(own, axes, high)]
    pallas_call x0 -> x2, Pallas kernels: none -> 15.5 us  [the longest x1 12 us: analysis(): pl.pallas_call(analysis_kernel, in_specs=[small] * 4 + [pl.BlockSpec(memo...]
    dot_general x35 -> x0, matrix products: 14.8 us -> none  [the longest x1 6.47 us: analyse(): jnp.dot(transform.T, ensemble, preferred_element_type=jnp.float32)]
    psum x1 -> x0, blocking collectives: 14.5 us -> none  [local(): total = lax.psum(total, 'lev')]
    unnamed x2 -> x10, local copies, waits for them, and re-layouts: 0.01 us -> 6.85 us
    reduce_sum x3 -> x0, other arithmetic: 4.13 us -> none  [the longest x1 3.39 us: analyse(): mean_state = jnp.mean(ensemble.astype(jnp.float32), axis=0)]
    ppermute x4 -> x5, starting transfers between devices: 9.41 us -> 11.7 us  [the longest x1 5.77 us: local(): from_far = lax.ppermute(to_far, axes, far)]
    another operation x3 -> x0, other arithmetic: 2.03 us -> none
  transfers between devices with their start and end apart: 4 -> 5, of which waited for: 1 -> 3; matrix products, arithmetic and copies ran while one was open for 5% -> 0% of each run, Pallas kernels for 0% -> 0%
where the time goes in v1:
time: 39.7 us; the launch traced here: 39.3 us
  Pallas kernels  15.5 us (39%)
  starting transfers between devices  11.7 us (29%)
  local copies, waits for them, and re-layouts  6.87 us (17%)
  waiting for transfers between devices  4.47 us (11%)
  between operations  0.69 us (2%)
    pallas_call x1, Pallas kernels, analysis(): pl.pallas_call(analysis_kernel, in_specs=[small] * 4 + [pl.BlockSpec(memo...  12 us
    unnamed x10, local copies, waits for them, and re-layouts  6.85 us
    ppermute x1, starting transfers between devices, local(): from_far = lax.ppermute(to_far, axes, far)  5.77 us
    pallas_call x1, Pallas kernels, grams(): pl.pallas_call(gram_kernel, grid=(GRAM_CHUNKS,), in_specs=[pl.BlockSpec(m...  3.54 us
    ppermute x1, starting transfers between devices, local(): from_near = lax.ppermute(to_near, axes, near)  2.88 us
    ppermute x1, waiting for transfers between devices, local(): other = lax.ppermute(own, axes, high)  2.17 us
    ppermute x1, starting transfers between devices, local(): other = lax.ppermute(own, axes, high)  1.55 us
    ppermute x1, starting transfers between devices, local(): gram = gram + lax.ppermute(gram, axes, core)  1.51 us
  transfers between devices with their start and end apart: 5, of which 3 were waited for; matrix products, arithmetic and copies ran while one was open for 0% of the time, Pallas kernels for 0%

profile of v1, /device:TPU:1, one launch (start us, length us, event | category | flops | bytes accessed | tf_op | source)
XLA Modules:
  0.0 39.3 jit_solution(6414963225247867435)
XLA Ops:
  0.7 0.1 pad_add_fusion.info
  0.7 0.0 copy-start.1
  0.7 1.7 %copy-done.1 = bf16[80,16384]{1,0:T(8,128)(2,1)S(1)} copy-done((bf16[80,16384]{1,0:T(8,128)(2,1)S(1)}, bf16[80,16384]{1,0:T(8,128)(2,1)}, u32[]{:S(2)}) %copy-start.1) | copy-done | bytes 2621464
  2.5 0.0 copy-start.2
  2.5 0.9 %copy-done.2 = f32[3,16384]{1,0:T(4,128)S(1)} copy-done((f32[3,16384]{1,0:T(4,128)S(1)}, f32[3,16384]{1,0:T(4,128)}, u32[]{:S(2)}) %copy-start.2) | copy-done | bytes 196632
  3.4 0.0 copy-start.3
  3.4 0.8 %copy-done.3 = f32[16384]{0:T(1024)S(1)} copy-done((f32[16384]{0:T(1024)S(1)}, f32[16384]{0:T(1024)}, u32[]{:S(2)}) %copy-start.3) | copy-done | bytes 65560
  4.3 0.0 copy-start.4
  4.3 0.8 %copy-done.4 = f32[16384]{0:T(1024)S(1)} copy-done((f32[16384]{0:T(1024)S(1)}, f32[16384]{0:T(1024)}, u32[]{:S(2)}) %copy-start.4) | copy-done | bytes 65560
  5.1 3.5 %grams.1 = f32[240,128]{1,0:T(8,128)S(1)} custom-call(s32[2]{0:T(128)S(1)} %pad_add_fusion.info, bf16[80,16384]{1,0:T(8,128)(2,1)S(1)} %copy-done.1, f32[1,16384]{1,0:T(1,128)S(1)} %bitcast.3, f32[1,16384]{1,0:T(1,128)S(1)} %bitcast.4, f32[3,16384]{1,0:T(4,128)S(1)} %copy-done.2), custom_call_target="tpu_custom_call" | custom-call | tf_op jit(solution)/shard_map/grams/pallas_call | solution.py:47
  8.6 1.5 %collective-permute-start = (f32[240,128]{1,0:T(8,128)S(1)}, f32[240,128]{1,0:T(8,128)S(1)}, u32[]{:S(2)}, u32[]{:S(2)}) collective-permute-start(f32[240,128]{1,0:T(8,128)S(1)} %grams.1), channel_id=1, source_target_pairs={{0,1},{1,0},{2,3},{3,2},{4,5},{5,4},{6,7},{7,6},{8,9},{9,8},{10,11... | collective-permute-start | bytes 368648 | tf_op jit(solution)/shard_map/ppermute | solution.py:166
  10.2 1.0 %collective-permute-done = f32[240,128]{1,0:T(8,128)S(1)} collective-permute-done((f32[240,128]{1,0:T(8,128)S(1)}, f32[240,128]{1,0:T(8,128)S(1)}, u32[]{:S(2)}, u32[]{:S(2)}) %collective-permute-start) | collective-permute-done | bytes 122912 | tf_op jit(solution)/shard_map/ppermute | solution.py:166
  11.2 2.9 %collective-permute-start.3 = (f32[80,128]{1,0:T(8,128)S(1)}, f32[80,128]{1,0:T(8,128)S(1)}, u32[]{:S(2)}, u32[]{:S(2)}) collective-permute-start(f32[80,128]{1,0:T(8,128)S(1)} %get-tuple-element.5), channel_id=1, source_target_pairs={{0,4},{1,7},{2,6},{3,5},{4,0},{5,3},{6,2},{7,1},{8,12},{9,15},{10,... | collective-permute-start | bytes 122888 | tf_op jit(solution)/shard_map/ppermute | solution.py:169
  14.1 5.8 %collective-permute-start.2 = (f32[80,128]{1,0:T(8,128)S(1)}, f32[80,128]{1,0:T(8,128)S(1)}, u32[]{:S(2)}, u32[]{:S(2)}) collective-permute-start(f32[80,128]{1,0:T(8,128)S(1)} %get-tuple-element.6), channel_id=1, source_target_pairs={{0,124},{1,127},{2,126},{3,125},{4,8},{5,11},{6,10},{7,9},{8,4},{9... | collective-permute-start | bytes 122888 | tf_op jit(solution)/shard_map/ppermute | solution.py:168
  19.8 1.6 %collective-permute-start.1 = (f32[80,128]{1,0:T(8,128)S(1)}, f32[80,128]{1,0:T(8,128)S(1)}, u32[]{:S(2)}, u32[]{:S(2)}) collective-permute-start(f32[80,128]{1,0:T(8,128)S(1)} %get-tuple-element.7.own), channel_id=1, source_target_pairs={{0,2},{1,3},{2,0},{3,1},{4,6},{5,7},{6,4},{7,5},{8,10},{9,11},{10,... | collective-permute-start | bytes 122888 | tf_op jit(solution)/shard_map/ppermute | solution.py:170
  21.4 0.0 collective-permute-done.3
  21.4 1.3 %collective-permute-done.2 = f32[80,128]{1,0:T(8,128)S(1)} collective-permute-done((f32[80,128]{1,0:T(8,128)S(1)}, f32[80,128]{1,0:T(8,128)S(1)}, u32[]{:S(2)}, u32[]{:S(2)}) %collective-permute-start.2) | collective-permute-done | bytes 40992 | tf_op jit(solution)/shard_map/ppermute | solution.py:168
  22.7 0.0 collective-permute-start.4
  22.7 2.2 %collective-permute-done.1.other = f32[80,128]{1,0:T(8,128)S(1)} collective-permute-done((f32[80,128]{1,0:T(8,128)S(1)}, f32[80,128]{1,0:T(8,128)S(1)}, u32[]{:S(2)}, u32[]{:S(2)}) %collective-permute-start.1) | collective-permute-done | bytes 40992 | tf_op jit(solution)/shard_map/ppermute | solution.py:170
  24.9 0.0 collective-permute-done.4.theirs
  24.9 0.0 copy-start
  24.9 2.5 %copy-done = bf16[80,32768]{1,0:T(8,128)(2,1)S(1)} copy-done((bf16[80,32768]{1,0:T(8,128)(2,1)S(1)}, bf16[80,32768]{1,0:T(8,128)(2,1)}, u32[]{:S(2)}) %copy-start) | copy-done | bytes 5242904
  27.4 12.0 %analysis.1 = bf16[80,32768]{1,0:T(8,128)(2,1)} custom-call(f32[80,128]{1,0:T(8,128)S(1)} %get-tuple-element.7.own, f32[80,128]{1,0:T(8,128)S(1)} %collective-permute-done.1.other, f32[80,128]{1,0:T(8,128)S(1)} %add.7.mine, f32[80,128]{1,0:T(8,128)S(1)} %collective-permute-done.4.theirs, bf16[80,32768]{1,0:T(8,128)(2,1)S(1)} %copy-done), custom_call_target="tpu_custom_call" | custom-call | tf_op jit(solution)/shard_map/analysis/pallas_call | solution.py:130
  (3 shorter events, 0.0 us)
Async XLA Ops:
  0.7 1.7 %copy-start.1 = (bf16[80,16384]{1,0:T(8,128)(2,1)S(1)}, bf16[80,16384]{1,0:T(8,128)(2,1)}, u32[]{:S(2)}) copy-start(bf16[80,16384]{1,0:T(8,128)(2,1)} %pert.1) | copy-start | bytes 7864324
  2.5 0.9 %copy-start.2 = (f32[3,16384]{1,0:T(4,128)S(1)}, f32[3,16384]{1,0:T(4,128)}, u32[]{:S(2)}) copy-start(f32[3,16384]{1,0:T(4,128)} %loc.1) | copy-start | bytes 589828
  3.4 0.8 %copy-start.3 = (f32[16384]{0:T(1024)S(1)}, f32[16384]{0:T(1024)}, u32[]{:S(2)}) copy-start(f32[16384]{0:T(1024)} %param.8) | copy-start | bytes 196612
  4.3 0.8 %copy-start.4 = (f32[16384]{0:T(1024)S(1)}, f32[16384]{0:T(1024)}, u32[]{:S(2)}) copy-start(f32[16384]{0:T(1024)} %param.9) | copy-start | bytes 196612
  8.6 2.5 %collective-permute-start = (f32[240,128]{1,0:T(8,128)S(1)}, f32[240,128]{1,0:T(8,128)S(1)}, u32[]{:S(2)}, u32[]{:S(2)}) collective-permute-start(f32[240,128]{1,0:T(8,128)S(1)} %grams.1), channel_id=1, source_target_pairs={{0,1},{1,0},{2,3},{3,2},{4,5},{5,4},{6,7},{7,6},{8,9},{9,8},{10,11... | collective-permute-start | bytes 368648 | tf_op jit(solution)/shard_map/ppermute | solution.py:166
  11.2 10.2 %collective-permute-start.3 = (f32[80,128]{1,0:T(8,128)S(1)}, f32[80,128]{1,0:T(8,128)S(1)}, u32[]{:S(2)}, u32[]{:S(2)}) collective-permute-start(f32[80,128]{1,0:T(8,128)S(1)} %get-tuple-element.5), channel_id=1, source_target_pairs={{0,4},{1,7},{2,6},{3,5},{4,0},{5,3},{6,2},{7,1},{8,12},{9,15},{10,... | collective-permute-start | bytes 122888 | tf_op jit(solution)/shard_map/ppermute | solution.py:169
  14.1 8.7 %collective-permute-start.2 = (f32[80,128]{1,0:T(8,128)S(1)}, f32[80,128]{1,0:T(8,128)S(1)}, u32[]{:S(2)}, u32[]{:S(2)}) collective-permute-start(f32[80,128]{1,0:T(8,128)S(1)} %get-tuple-element.6), channel_id=1, source_target_pairs={{0,124},{1,127},{2,126},{3,125},{4,8},{5,11},{6,10},{7,9},{8,4},{9... | collective-permute-start | bytes 122888 | tf_op jit(solution)/shard_map/ppermute | solution.py:168
  19.8 5.1 %collective-permute-start.1 = (f32[80,128]{1,0:T(8,128)S(1)}, f32[80,128]{1,0:T(8,128)S(1)}, u32[]{:S(2)}, u32[]{:S(2)}) collective-permute-start(f32[80,128]{1,0:T(8,128)S(1)} %get-tuple-element.7.own), channel_id=1, source_target_pairs={{0,2},{1,3},{2,0},{3,1},{4,6},{5,7},{6,4},{7,5},{8,10},{9,11},{10,... | collective-permute-start | bytes 122888 | tf_op jit(solution)/shard_map/ppermute | solution.py:170
  22.7 2.2 %collective-permute-start.4 = (f32[80,128]{1,0:T(8,128)S(1)}, f32[80,128]{1,0:T(8,128)S(1)}, u32[]{:S(2)}, u32[]{:S(2)}) collective-permute-start(f32[80,128]{1,0:T(8,128)S(1)} %add.7.mine), channel_id=1, source_target_pairs={{0,1},{1,0},{2,3},{3,2},{4,5},{5,4},{6,7},{7,6},{8,9},{9,8},{10,11... | collective-permute-start | bytes 122888 | tf_op jit(solution)/shard_map/ppermute | solution.py:172
  24.9 2.5 %copy-start = (bf16[80,32768]{1,0:T(8,128)(2,1)S(1)}, bf16[80,32768]{1,0:T(8,128)(2,1)}, u32[]{:S(2)}) copy-start(bf16[80,32768]{1,0:T(8,128)(2,1)} %ensemble.1) | copy-start | bytes 15728644

commit v2 on v1

v2 whole, which is shorter than its diff:
```python
import functools
import math

import jax
import jax.numpy as jnp
from jax import lax
from jax.experimental import pallas as pl
from jax.experimental.pallas import tpu as pltpu
from jax.sharding import PartitionSpec as P

NS_STEPS = 10
OBS_CHUNKS = 2
FETCHES = 4
STORES = (2048, 2048, 4096, 8192, 8192, 4096, 2048, 2048)
VMEM_BYTES = 40 * 1024 * 1024


def in_hbm(array):
    return pltpu.with_memory_space_constraint(array, pltpu.HBM)


def gram_kernel(
    count, parity, pert, innov, rinv, loc, out, pert_in, innov_in, rinv_in, loc_in, pert_sem, sem
):
    members, width = pert_in.shape
    chunk = width // OBS_CHUNKS
    sides = [
        pltpu.make_async_copy(source, target, sem.at[i])
        for i, (source, target) in enumerate(((rinv, rinv_in), (loc, loc_in), (innov, innov_in)))
    ]
    blocks = []
    for i in range(OBS_CHUNKS):
        part = pl.ds(i * chunk, chunk)
        blocks.append(pltpu.make_async_copy(pert.at[:, part], pert_in.at[:, part], pert_sem.at[i]))
    for copy in sides + blocks:
        copy.start()
    for copy in sides:
        copy.wait()
    even = parity[0] == 0
    total = None
    for i in range(OBS_CHUNKS):
        part = pl.ds(i * chunk, chunk)
        slots = i * chunk + lax.broadcasted_iota(jnp.int32, (1, chunk), 1)
        live = (slots < count[0]).astype(jnp.float32)
        scaled = rinv_in[:, part]
        before, own, after = [
            (scaled * loc_in[j : j + 1, part] * live).astype(jnp.bfloat16) for j in range(3)
        ]
        near = jnp.where(even, after, before)
        far = jnp.where(even, before, after)
        side = jnp.broadcast_to(innov_in[:, part].astype(jnp.bfloat16), (16, chunk))
        blocks[i].wait()
        block = pert_in[:, part]
        left = jnp.concatenate([block * far, block * near, block * own], axis=0)
        right = jnp.concatenate([block, side], axis=0)
        gram = lax.dot_general(
            left, right, (((1,), (1,)), ((), ())), preferred_element_type=jnp.float32
        )
        total = gram if total is None else total + gram
    out[:, : members + 16] = total
    out[:, members + 16 :] = jnp.zeros((3 * members, 112 - members), jnp.float32)


def grams(pert, innov, rinv, loc, count, parity):
    members, width = pert.shape
    return pl.pallas_call(
        gram_kernel,
        in_specs=[pl.BlockSpec(memory_space=pltpu.SMEM)] * 2
        + [pl.BlockSpec(memory_space=pltpu.HBM)] * 4,
        out_specs=pl.BlockSpec(memory_space=pltpu.VMEM),
        out_shape=jax.ShapeDtypeStruct((3 * members, 128), jnp.float32),
        scratch_shapes=[
            pltpu.VMEM((members, width), jnp.bfloat16),
            pltpu.VMEM((1, width), jnp.float32),
            pltpu.VMEM((1, width), jnp.float32),
            pltpu.VMEM((3, width), jnp.float32),
            pltpu.SemaphoreType.DMA((OBS_CHUNKS,)),
            pltpu.SemaphoreType.DMA((3,)),
        ],
        compiler_params=pltpu.CompilerParams(vmem_limit_bytes=VMEM_BYTES),
        name="grams",
    )(count, parity, *(in_hbm(x) for x in (pert, innov, rinv, loc)))


def exact(a, b):
    return jnp.dot(a, b, precision=lax.Precision.HIGHEST, preferred_element_type=jnp.float32)


def transform_of(total):
    members = total.shape[0]
    rows = lax.broadcasted_iota(jnp.int32, total.shape, 0)
    cols = lax.broadcasted_iota(jnp.int32, total.shape, 1)
    eye = (rows == cols).astype(jnp.float32)[:, :members]
    mat = (members - 1.0) * eye + total[:, :members]
    scale = jnp.sqrt(jnp.sum(mat * mat))
    iterate = mat / scale
    factor = 1.5 * eye - 0.5 * iterate
    inverse_root = factor
    iterate = exact(iterate, factor)
    for _ in range(NS_STEPS - 1):
        factor = 1.5 * eye - 0.5 * exact(inverse_root, iterate)
        iterate = exact(iterate, factor)
        inverse_root = exact(factor, inverse_root)
    root_inv = inverse_root / jnp.sqrt(scale)
    mean_weight = exact(root_inv, exact(root_inv, total))[:, members : members + 1]
    transform = (math.sqrt(members - 1.0) * root_inv + mean_weight).astype(jnp.bfloat16)
    flipped = transform.astype(jnp.float32).T
    keep = 1.0 - jnp.sum(flipped, axis=1, keepdims=True)
    return flipped + keep / members


def analysis_kernel(own, other, mine, theirs, ensemble, out, held, result, in_sem, out_sem):
    members, width = held.shape
    chunk = width // FETCHES
    fetches, stores, parts = [], [], []
    for i in range(FETCHES):
        part = pl.ds(i * chunk, chunk)
        fetches.append(pltpu.make_async_copy(ensemble.at[:, part], held.at[:, part], in_sem.at[i]))
    for i, length in enumerate(STORES):
        part = pl.ds(sum(STORES[:i]), length)
        parts.append(part)
        stores.append(pltpu.make_async_copy(result.at[:, part], out.at[:, part], out_sem.at[i]))
    for copy in fetches:
        copy.start()
    weights = transform_of(own[...] + other[...] + mine[...] + theirs[...])
    high = weights.astype(jnp.bfloat16)
    low = (weights - high.astype(jnp.float32)).astype(jnp.bfloat16)
    left = jnp.concatenate([high, low], axis=1)
    for copy in fetches:
        copy.wait()
    for part, copy in zip(parts, stores):
        block = held[:, part]
        both = jnp.concatenate([block, block], axis=0)
        result[:, part] = jnp.dot(left, both, preferred_element_type=jnp.float32).astype(
            jnp.bfloat16
        )
        copy.start()
    for copy in stores:
        copy.wait()


def analysis(own, other, mine, theirs, ensemble):
    members, width = ensemble.shape
    assert sum(STORES) == width
    return pl.pallas_call(
        analysis_kernel,
        in_specs=[pl.BlockSpec(memory_space=pltpu.VMEM)] * 4 + [pl.BlockSpec(memory_space=pltpu.HBM)],
        out_specs=pl.BlockSpec(memory_space=pltpu.HBM),
        out_shape=jax.ShapeDtypeStruct((members, width), jnp.bfloat16),
        scratch_shapes=[
            pltpu.VMEM((members, width), jnp.bfloat16),
            pltpu.VMEM((members, width), jnp.bfloat16),
            pltpu.SemaphoreType.DMA((FETCHES,)),
            pltpu.SemaphoreType.DMA((len(STORES),)),
        ],
        compiler_params=pltpu.CompilerParams(vmem_limit_bytes=VMEM_BYTES),
        name="analysis",
    )(own, other, mine, theirs, in_hbm(ensemble))


def local(n_tile, n_lev, ensemble, obs_pert, innovation, obs_rinv, loc_weight, obs_count):
    members = obs_pert.shape[0]
    axes = ("tile", "lev")

    def pairs(partner):
        return [
            (t * n_lev + l, (lambda a, b: a * n_lev + b)(*partner(t, l)))
            for t in range(n_tile)
            for l in range(n_lev)
        ]

    core = pairs(lambda t, l: (t, l ^ 1))
    high = pairs(lambda t, l: (t, l ^ 2))
    near = pairs(lambda t, l: (t ^ 1, l ^ (2 * (l & 1))))
    far = pairs(lambda t, l: ((t + 1 if t & 1 else t - 1) % n_tile, l ^ (2 * (l & 1))))

    parity = lax.rem(lax.axis_index("tile"), 2).astype(jnp.int32)
    gram = grams(
        obs_pert, innovation[None, :], obs_rinv[None, :], loc_weight, obs_count, parity[None]
    )
    gram = gram + lax.ppermute(gram, axes, core)
    to_far, to_near, own = gram[:members], gram[members : 2 * members], gram[2 * members :]
    from_far = lax.ppermute(to_far, axes, far)
    from_near = lax.ppermute(to_near, axes, near)
    other = lax.ppermute(own, axes, high)
    mine = from_far + from_near
    theirs = lax.ppermute(mine, axes, core)
    return analysis(own, other, mine, theirs, ensemble)


def solution(mesh):
    return jax.shard_map(
        functools.partial(local, mesh.shape["tile"], mesh.shape["lev"]),
        mesh=mesh,
        in_specs=(
            P(None, ("tile", "lev")),
            P(None, ("tile", "lev")),
            P(("tile", "lev")),
            P(("tile", "lev")),
            P(None, ("tile", "lev")),
            P(("tile", "lev")),
        ),
        out_specs=P(None, ("tile", "lev")),
        check_vma=False,
    )
```

time: 39.7 us -> 28.7 us (0.72)
  local copies, waits for them, and re-layouts: 6.87 us -> 0.01 us
  Pallas kernels: 15.5 us -> 11.7 us
    unnamed x10 -> x0, local copies, waits for them, and re-layouts: 6.85 us -> none
    pallas_call x2, Pallas kernels: 15.5 us -> 11.7 us  [the longest x1 7.33 us: analysis(): pl.pallas_call(analysis_kernel, in_specs=[pl.BlockSpec(memory_space=pltpu...]
where the time goes in v2:
time: 28.7 us; the launch traced here: 28.6 us
  Pallas kernels  11.7 us (41%)
  starting transfers between devices  11.7 us (41%)
  waiting for transfers between devices  4.48 us (16%)
  between operations  0.68 us (2%)
    pallas_call x1, Pallas kernels, analysis(): pl.pallas_call(analysis_kernel, in_specs=[pl.BlockSpec(memory_space=pltpu...  7.33 us
    ppermute x1, starting transfers between devices, local(): from_far = lax.ppermute(to_far, axes, far)  5.76 us
    pallas_call x1, Pallas kernels, grams(): pl.pallas_call(gram_kernel, in_specs=[pl.BlockSpec(memory_space=pltpu.SME...  4.37 us
    ppermute x1, starting transfers between devices, local(): from_near = lax.ppermute(to_near, axes, near)  2.9 us
    ppermute x1, waiting for transfers between devices, local(): other = lax.ppermute(own, axes, high)  2.15 us
    ppermute x1, starting transfers between devices, local(): other = lax.ppermute(own, axes, high)  1.55 us
    ppermute x1, starting transfers between devices, local(): gram = gram + lax.ppermute(gram, axes, core)  1.5 us
    ppermute x1, waiting for transfers between devices, local(): from_far = lax.ppermute(to_far, axes, far)  1.34 us
  transfers between devices with their start and end apart: 5, of which 3 were waited for; matrix products, arithmetic and copies ran while one was open for 0% of the time, Pallas kernels for 0%

profile of v2, /device:TPU:1, one launch (start us, length us, event | category | flops | bytes accessed | tf_op | source)
XLA Modules:
  0.0 28.6 jit_solution(6791320210355668189)
XLA Ops:
  0.7 4.4 %grams.1 = f32[240,128]{1,0:T(8,128)S(1)} custom-call(s32[1]{0:T(128)S(6)} %copy.7.count, s32[1]{0:T(128)} %bitcast.parity, bf16[80,16384]{1,0:T(8,128)(2,1)} %pert.1, f32[1,16384]{1,0:T(1,128)} %bitcast.3, f32[1,16384]{1,0:T(1,128)} %bitcast.4, f32[3,16384]{1,0:T(4,128)} %loc.1), custom_call_target="tpu_custom_call" | custom-call | tf_op jit(solution)/shard_map/grams/pallas_call | solution.py:66
  5.0 1.5 %collective-permute-start = (f32[240,128]{1,0:T(8,128)S(1)}, f32[240,128]{1,0:T(8,128)S(1)}, u32[]{:S(2)}, u32[]{:S(2)}) collective-permute-start(f32[240,128]{1,0:T(8,128)S(1)} %grams.1), channel_id=1, source_target_pairs={{0,1},{1,0},{2,3},{3,2},{4,5},{5,4},{6,7},{7,6},{8,9},{9,8},{10,11... | collective-permute-start | bytes 368648 | tf_op jit(solution)/shard_map/ppermute | solution.py:181
  6.5 1.0 %collective-permute-done = f32[240,128]{1,0:T(8,128)S(1)} collective-permute-done((f32[240,128]{1,0:T(8,128)S(1)}, f32[240,128]{1,0:T(8,128)S(1)}, u32[]{:S(2)}, u32[]{:S(2)}) %collective-permute-start) | collective-permute-done | bytes 122912 | tf_op jit(solution)/shard_map/ppermute | solution.py:181
  7.5 2.9 %collective-permute-start.3 = (f32[80,128]{1,0:T(8,128)S(1)}, f32[80,128]{1,0:T(8,128)S(1)}, u32[]{:S(2)}, u32[]{:S(2)}) collective-permute-start(f32[80,128]{1,0:T(8,128)S(1)} %get-tuple-element.5), channel_id=1, source_target_pairs={{0,4},{1,7},{2,6},{3,5},{4,0},{5,3},{6,2},{7,1},{8,12},{9,15},{10,... | collective-permute-start | bytes 122888 | tf_op jit(solution)/shard_map/ppermute | solution.py:184
  10.4 5.8 %collective-permute-start.2 = (f32[80,128]{1,0:T(8,128)S(1)}, f32[80,128]{1,0:T(8,128)S(1)}, u32[]{:S(2)}, u32[]{:S(2)}) collective-permute-start(f32[80,128]{1,0:T(8,128)S(1)} %get-tuple-element.6), channel_id=1, source_target_pairs={{0,124},{1,127},{2,126},{3,125},{4,8},{5,11},{6,10},{7,9},{8,4},{9... | collective-permute-start | bytes 122888 | tf_op jit(solution)/shard_map/ppermute | solution.py:183
  16.2 1.6 %collective-permute-start.1 = (f32[80,128]{1,0:T(8,128)S(1)}, f32[80,128]{1,0:T(8,128)S(1)}, u32[]{:S(2)}, u32[]{:S(2)}) collective-permute-start(f32[80,128]{1,0:T(8,128)S(1)} %get-tuple-element.7.own), channel_id=1, source_target_pairs={{0,2},{1,3},{2,0},{3,1},{4,6},{5,7},{6,4},{7,5},{8,10},{9,11},{10,... | collective-permute-start | bytes 122888 | tf_op jit(solution)/shard_map/ppermute | solution.py:185
  17.8 0.0 collective-permute-done.3
  17.8 1.3 %collective-permute-done.2 = f32[80,128]{1,0:T(8,128)S(1)} collective-permute-done((f32[80,128]{1,0:T(8,128)S(1)}, f32[80,128]{1,0:T(8,128)S(1)}, u32[]{:S(2)}, u32[]{:S(2)}) %collective-permute-start.2) | collective-permute-done | bytes 40992 | tf_op jit(solution)/shard_map/ppermute | solution.py:183
  19.1 0.0 collective-permute-start.4
  19.1 2.2 %collective-permute-done.1.other = f32[80,128]{1,0:T(8,128)S(1)} collective-permute-done((f32[80,128]{1,0:T(8,128)S(1)}, f32[80,128]{1,0:T(8,128)S(1)}, u32[]{:S(2)}, u32[]{:S(2)}) %collective-permute-start.1) | collective-permute-done | bytes 40992 | tf_op jit(solution)/shard_map/ppermute | solution.py:185
  21.3 0.0 collective-permute-done.4.theirs
  21.3 7.3 %analysis.1 = bf16[80,32768]{1,0:T(8,128)(2,1)} custom-call(f32[80,128]{1,0:T(8,128)S(1)} %get-tuple-element.7.own, f32[80,128]{1,0:T(8,128)S(1)} %collective-permute-done.1.other, f32[80,128]{1,0:T(8,128)S(1)} %add.7.mine, f32[80,128]{1,0:T(8,128)S(1)} %collective-permute-done.4.theirs, bf16[80,32768]{1,0:T(8,128)(2,1)} %ensemble.1), custom_call_target="tpu_custom_call" | custom-call | tf_op jit(solution)/shard_map/analysis/pallas_call | solution.py:145
  (3 shorter events, 0.0 us)
Async XLA Ops:
  5.0 2.5 %collective-permute-start = (f32[240,128]{1,0:T(8,128)S(1)}, f32[240,128]{1,0:T(8,128)S(1)}, u32[]{:S(2)}, u32[]{:S(2)}) collective-permute-start(f32[240,128]{1,0:T(8,128)S(1)} %grams.1), channel_id=1, source_target_pairs={{0,1},{1,0},{2,3},{3,2},{4,5},{5,4},{6,7},{7,6},{8,9},{9,8},{10,11... | collective-permute-start | bytes 368648 | tf_op jit(solution)/shard_map/ppermute | solution.py:181
  7.5 10.2 %collective-permute-start.3 = (f32[80,128]{1,0:T(8,128)S(1)}, f32[80,128]{1,0:T(8,128)S(1)}, u32[]{:S(2)}, u32[]{:S(2)}) collective-permute-start(f32[80,128]{1,0:T(8,128)S(1)} %get-tuple-element.5), channel_id=1, source_target_pairs={{0,4},{1,7},{2,6},{3,5},{4,0},{5,3},{6,2},{7,1},{8,12},{9,15},{10,... | collective-permute-start | bytes 122888 | tf_op jit(solution)/shard_map/ppermute | solution.py:184
  10.4 8.7 %collective-permute-start.2 = (f32[80,128]{1,0:T(8,128)S(1)}, f32[80,128]{1,0:T(8,128)S(1)}, u32[]{:S(2)}, u32[]{:S(2)}) collective-permute-start(f32[80,128]{1,0:T(8,128)S(1)} %get-tuple-element.6), channel_id=1, source_target_pairs={{0,124},{1,127},{2,126},{3,125},{4,8},{5,11},{6,10},{7,9},{8,4},{9... | collective-permute-start | bytes 122888 | tf_op jit(solution)/shard_map/ppermute | solution.py:183
  16.2 5.1 %collective-permute-start.1 = (f32[80,128]{1,0:T(8,128)S(1)}, f32[80,128]{1,0:T(8,128)S(1)}, u32[]{:S(2)}, u32[]{:S(2)}) collective-permute-start(f32[80,128]{1,0:T(8,128)S(1)} %get-tuple-element.7.own), channel_id=1, source_target_pairs={{0,2},{1,3},{2,0},{3,1},{4,6},{5,7},{6,4},{7,5},{8,10},{9,11},{10,... | collective-permute-start | bytes 122888 | tf_op jit(solution)/shard_map/ppermute | solution.py:185
  19.1 2.2 %collective-permute-start.4 = (f32[80,128]{1,0:T(8,128)S(1)}, f32[80,128]{1,0:T(8,128)S(1)}, u32[]{:S(2)}, u32[]{:S(2)}) collective-permute-start(f32[80,128]{1,0:T(8,128)S(1)} %add.7.mine), channel_id=1, source_target_pairs={{0,1},{1,0},{2,3},{3,2},{4,5},{5,4},{6,7},{7,6},{8,9},{9,8},{10,11... | collective-permute-start | bytes 122888 | tf_op jit(solution)/shard_map/ppermute | solution.py:187

commit v3 on v2

v3 whole, which is shorter than its diff:
```python
import functools
import math

import jax
import jax.numpy as jnp
from jax import lax
from jax.experimental import pallas as pl
from jax.experimental.pallas import tpu as pltpu
from jax.sharding import PartitionSpec as P

NS_STEPS = 10
OBS_CHUNKS = 2
SIDE_ROWS = 16
FETCHES = 4
STORES = (2048, 2048, 4096, 8192, 8192, 4096, 2048, 2048)
VMEM_BYTES = 40 * 1024 * 1024


def in_hbm(array):
    return pltpu.with_memory_space_constraint(array, pltpu.HBM)


def weighted_grams(rows, right):
    members = right.shape[0] - SIDE_ROWS
    left = jnp.concatenate([right[:members] * row for row in rows], axis=0)
    return lax.dot_general(left, right, (((1,), (1,)), ((), ())), preferred_element_type=jnp.float32)


def widened(gram):
    return jnp.concatenate(
        [gram, jnp.zeros((gram.shape[0], 128 - gram.shape[1]), jnp.float32)], axis=1
    )


def outer_kernel(
    count, place, pert, innov, rinv, loc, out, right, own, innov_in, rinv_in, loc_in, pert_sem, sem
):
    members, width = pert.shape
    chunk = width // OBS_CHUNKS
    sides = [
        pltpu.make_async_copy(source, target, sem.at[i])
        for i, (source, target) in enumerate(((rinv, rinv_in), (loc, loc_in), (innov, innov_in)))
    ]
    blocks = []
    for i in range(OBS_CHUNKS):
        part = pl.ds(i * chunk, chunk)
        target = right.at[pl.ds(0, members), part]
        blocks.append(pltpu.make_async_copy(pert.at[:, part], target, pert_sem.at[i]))
    for copy in sides + blocks:
        copy.start()
    for copy in sides:
        copy.wait()
    even = place[0] == 0
    total = None
    for i in range(OBS_CHUNKS):
        part = pl.ds(i * chunk, chunk)
        slots = i * chunk + lax.broadcasted_iota(jnp.int32, (1, chunk), 1)
        live = (slots < count[0]).astype(jnp.float32)
        scaled = rinv_in[:, part]
        before, mid, after = [
            (scaled * loc_in[j : j + 1, part] * live).astype(jnp.bfloat16) for j in range(3)
        ]
        own[:, part] = mid
        right[members:, part] = jnp.broadcast_to(
            innov_in[:, part].astype(jnp.bfloat16), (SIDE_ROWS, chunk)
        )
        rows = (jnp.where(even, before, after), jnp.where(even, after, before))
        blocks[i].wait()
        gram = weighted_grams(rows, right[:, part])
        total = gram if total is None else total + gram
    out[...] = widened(total)


def outer_grams(pert, innov, rinv, loc, count, place):
    members, width = pert.shape
    return pl.pallas_call(
        outer_kernel,
        in_specs=[pl.BlockSpec(memory_space=pltpu.SMEM)] * 2
        + [pl.BlockSpec(memory_space=pltpu.HBM)] * 4,
        out_specs=[pl.BlockSpec(memory_space=pltpu.VMEM)] * 3,
        out_shape=[
            jax.ShapeDtypeStruct((2 * members, 128), jnp.float32),
            jax.ShapeDtypeStruct((members + SIDE_ROWS, width), jnp.bfloat16),
            jax.ShapeDtypeStruct((1, width), jnp.bfloat16),
        ],
        scratch_shapes=[
            pltpu.VMEM((1, width), jnp.float32),
            pltpu.VMEM((1, width), jnp.float32),
            pltpu.VMEM((3, width), jnp.float32),
            pltpu.SemaphoreType.DMA((OBS_CHUNKS,)),
            pltpu.SemaphoreType.DMA((3,)),
        ],
        compiler_params=pltpu.CompilerParams(vmem_limit_bytes=VMEM_BYTES),
        name="outer_grams",
    )(count, place, *(in_hbm(x) for x in (pert, innov, rinv, loc)))


def own_kernel(right, own, out):
    out[...] = widened(weighted_grams((own[...],), right[...]))


def own_gram(right, own):
    members = right.shape[0] - SIDE_ROWS
    width = right.shape[1]
    return pl.pallas_call(
        own_kernel,
        in_specs=[pl.BlockSpec(memory_space=pltpu.VMEM)] * 2,
        out_specs=pl.BlockSpec(memory_space=pltpu.VMEM),
        out_shape=jax.ShapeDtypeStruct((members, 128), jnp.float32),
        compiler_params=pltpu.CompilerParams(vmem_limit_bytes=VMEM_BYTES),
        cost_estimate=pl.CostEstimate(
            flops=2 * members * 128 * width, bytes_accessed=2 * right.size, transcendentals=0
        ),
        name="own_gram",
    )(right, own)


def split(array):
    high = array.astype(jnp.bfloat16)
    rest = array - high.astype(jnp.float32)
    middle = rest.astype(jnp.bfloat16)
    return high, middle, (rest - middle.astype(jnp.float32)).astype(jnp.bfloat16)


def dot(a, b):
    return jnp.dot(a, b, preferred_element_type=jnp.float32)


def product(a, b):
    high, middle, low = a
    below = jnp.zeros((128 - b[0].shape[0], 128), jnp.bfloat16)
    b_high, b_middle, b_low = (jnp.concatenate([part, below], axis=0) for part in b)
    pair = jnp.concatenate([b_high, b_middle], axis=1)
    large = dot(jnp.concatenate([high, middle], axis=1), jnp.concatenate([pair, pair], axis=0))
    small = dot(jnp.concatenate([low, high], axis=1), jnp.concatenate([b_high, b_low], axis=0))
    return (small + large[:, 128:]) + large[:, :128]


def transform_of(total):
    members = total.shape[0]
    rows = lax.broadcasted_iota(jnp.int32, total.shape, 0)
    cols = lax.broadcasted_iota(jnp.int32, total.shape, 1)
    eye = (rows == cols).astype(jnp.float32)
    square = cols < members
    wide = jnp.where(cols <= members, total, 0.0) + (members - 1.0) * eye
    mat = jnp.where(square, wide, 0.0)
    proj = wide - mat
    parts = split(wide)
    squared = product(parts, parts)
    inv = 1.0 / jnp.sqrt(jnp.sum(mat * mat, keepdims=True))
    head = jnp.where(square, squared, 0.0)
    iterate = split((1.5 * inv) * mat - (0.5 * inv * inv) * head)
    inverse_root = 1.5 * (eye + proj) - (0.5 * inv) * (mat + (squared - head))
    for step in range(1, NS_STEPS):
        root_parts = split(inverse_root)
        factor = split(1.5 * eye - 0.5 * product(root_parts, iterate))
        if step < NS_STEPS - 1:
            iterate = split(product(iterate, factor))
        inverse_root = product(factor, root_parts)
    root = jnp.where(square, inverse_root, 0.0)
    mean_weight = inv * jnp.sum(
        root * inverse_root[:, members : members + 1], axis=0, keepdims=True
    )
    scaled = root * (math.sqrt(members - 1.0) * jnp.sqrt(inv))
    transform = (scaled + mean_weight).astype(jnp.bfloat16).astype(jnp.float32)[:, :members]
    keep = 1.0 - jnp.sum(transform, axis=1, keepdims=True)
    return transform + keep / members


def analysis_kernel(own, high, mine, theirs, ensemble, out, held, result, in_sem, out_sem):
    members, width = held.shape
    chunk = width // FETCHES
    fetches, stores, parts = [], [], []
    for i in range(FETCHES):
        part = pl.ds(i * chunk, chunk)
        fetches.append(pltpu.make_async_copy(ensemble.at[:, part], held.at[:, part], in_sem.at[i]))
    for i, length in enumerate(STORES):
        part = pl.ds(sum(STORES[:i]), length)
        parts.append(part)
        stores.append(pltpu.make_async_copy(result.at[:, part], out.at[:, part], out_sem.at[i]))
    for copy in fetches:
        copy.start()
    weights = transform_of((own[...] + high[...]) + (mine[...] + theirs[...]))
    high = weights.astype(jnp.bfloat16)
    low = (weights - high.astype(jnp.float32)).astype(jnp.bfloat16)
    left = jnp.concatenate([high, low], axis=1)
    for copy in fetches:
        copy.wait()
    for part, copy in zip(parts, stores):
        block = held[:, part]
        both = jnp.concatenate([block, block], axis=0)
        result[:, part] = jnp.dot(left, both, preferred_element_type=jnp.float32).astype(
            jnp.bfloat16
        )
        copy.start()
    for copy in stores:
        copy.wait()


def analysis(grams, ensemble):
    members, width = ensemble.shape
    assert sum(STORES) == width
    return pl.pallas_call(
        analysis_kernel,
        in_specs=[pl.BlockSpec(memory_space=pltpu.VMEM)] * len(grams) + [pl.BlockSpec(memory_space=pltpu.HBM)],
        out_specs=pl.BlockSpec(memory_space=pltpu.HBM),
        out_shape=jax.ShapeDtypeStruct((members, width), jnp.bfloat16),
        scratch_shapes=[
            pltpu.VMEM((members, width), jnp.bfloat16),
            pltpu.VMEM((members, width), jnp.bfloat16),
            pltpu.SemaphoreType.DMA((FETCHES,)),
            pltpu.SemaphoreType.DMA((len(STORES),)),
        ],
        compiler_params=pltpu.CompilerParams(vmem_limit_bytes=VMEM_BYTES),
        name="analysis",
    )(*grams, in_hbm(ensemble))


def local(n_tile, n_lev, ensemble, obs_pert, innovation, obs_rinv, loc_weight, obs_count):
    members = obs_pert.shape[0]
    axes = ("tile", "lev")

    def pairs(partner):
        return [
            (t * n_lev + l, (lambda a, b: a * n_lev + b)(*partner(t, l)))
            for t in range(n_tile)
            for l in range(n_lev)
        ]

    core = pairs(lambda t, l: (t, l ^ 1))
    high = pairs(lambda t, l: (t, l ^ 2))
    near = pairs(lambda t, l: (t ^ 1, l ^ (2 * (l & 1))))
    far = pairs(lambda t, l: ((t + 1 if t & 1 else t - 1) % n_tile, l ^ (2 * (l & 1))))
    place = (lax.axis_index("tile") % 2).astype(jnp.int32)
    outer, right, weight = outer_grams(
        obs_pert, innovation[None, :], obs_rinv[None, :], loc_weight, obs_count, place[None]
    )
    own = own_gram(right, weight)
    members = own.shape[0]
    outer = outer + lax.ppermute(outer, axes, core)
    own = own + lax.ppermute(own, axes, core)
    from_far = lax.ppermute(outer[:members], axes, far)
    from_near = lax.ppermute(outer[members:], axes, near)
    mine = from_far + from_near
    from_high = lax.ppermute(own, axes, high)
    return analysis((own, from_high, mine, lax.ppermute(mine, axes, core)), ensemble)


def solution(mesh):
    return jax.shard_map(
        functools.partial(local, mesh.shape["tile"], mesh.shape["lev"]),
        mesh=mesh,
        in_specs=(
            P(None, ("tile", "lev")),
            P(None, ("tile", "lev")),
            P(("tile", "lev")),
            P(("tile", "lev")),
            P(None, ("tile", "lev")),
            P(("tile", "lev")),
        ),
        out_specs=P(None, ("tile", "lev")),
        check_vma=False,
    )
```

time: 28.7 us -> 27 us (0.941)
  waiting for transfers between devices: 4.48 us -> 3.14 us
  Pallas kernels: 11.7 us -> 10.8 us
  starting transfers between devices: 11.7 us -> 12.2 us
    ppermute x5 -> x6, waiting for transfers between devices: 4.48 us -> 3.14 us  [the longest x1 1.98 us: local(): from_high = lax.ppermute(own, axes, high)]
    pallas_call x1, Pallas kernels: 7.33 us -> 6.3 us  [analysis(): pl.pallas_call(analysis_kernel, in_specs=[pl.BlockSpec(memory_space=pltpu...]
    ppermute x5 -> x6, starting transfers between devices: 11.7 us -> 12.2 us  [the longest x1 5.75 us: local(): from_far = lax.ppermute(outer[:members], axes, far)]
    pallas_call x1 -> x2, Pallas kernels: 4.37 us -> 4.55 us  [the longest x1 3.6 us: outer_grams(): pl.pallas_call(outer_kernel, in_specs=[pl.BlockSpec(memory_space=pltpu.SM...]
  transfers between devices with their start and end apart: 5 -> 6, of which waited for: 3 -> 2; matrix products, arithmetic and copies ran while one was open for 0% -> 0% of each run, Pallas kernels for 0% -> 4%
where the time goes in v3:
time: 27 us; the launch traced here: 26.9 us
  starting transfers between devices  12.2 us (45%)
  Pallas kernels  10.8 us (40%)
  waiting for transfers between devices  3.14 us (12%)
  between operations  0.7 us (3%)
    pallas_call x1, Pallas kernels, analysis(): pl.pallas_call(analysis_kernel, in_specs=[pl.BlockSpec(memory_space=pltpu...  6.3 us
    ppermute x1, starting transfers between devices, local(): from_far = lax.ppermute(outer[:members], axes, far)  5.75 us
    pallas_call x1, Pallas kernels, outer_grams(): pl.pallas_call(outer_kernel, in_specs=[pl.BlockSpec(memory_space=pltpu.SM...  3.6 us
    ppermute x1, starting transfers between devices, local(): from_near = lax.ppermute(outer[members:], axes, near)  2.92 us
    ppermute x1, waiting for transfers between devices, local(): from_high = lax.ppermute(own, axes, high)  1.98 us
    ppermute x1, starting transfers between devices, local(): from_high = lax.ppermute(own, axes, high)  1.63 us
    ppermute x1, starting transfers between devices, local(): outer = outer + lax.ppermute(outer, axes, core)  1.5 us
    ppermute x1, waiting for transfers between devices, local(): from_far = lax.ppermute(outer[:members], axes, far)  1.15 us
  transfers between devices with their start and end apart: 6, of which 2 were waited for; matrix products, arithmetic and copies ran while one was open for 0% of the time, Pallas kernels for 4%

profile of v3, /device:TPU:1, one launch (start us, length us, event | category | flops | bytes accessed | tf_op | source)
XLA Modules:
  0.0 26.9 jit_solution(15855806303911387607)
XLA Ops:
  0.7 3.6 %outer_grams.1 = (f32[160,128]{1,0:T(8,128)S(1)}, bf16[96,16384]{1,0:T(8,128)(2,1)S(1)}, bf16[1,16384]{1,0:T(2,128)(2,1)S(1)}) custom-call(s32[1]{0:T(128)S(6)} %copy.7.count, s32[1]{0:T(128)} %bitcast.place, bf16[80,16384]{1,0:T(8,128)(2,1)} %pert.1, f32[1,16384]{1,0:T(1,128)} %bitcast.3, f32[1,16384]{1,0:T(1,128)} %bitcast.4, f32[3,16384]{1,0:T(4,128)} %loc.1), custom_call_target="tpu_custom_call" | custom-call | tf_op jit(solution)/shard_map/outer_grams/pallas_call | solution.py:76
  4.3 1.5 %collective-permute-start.2 = (f32[160,128]{1,0:T(8,128)S(1)}, f32[160,128]{1,0:T(8,128)S(1)}, u32[]{:S(2)}, u32[]{:S(2)}) collective-permute-start(f32[160,128]{1,0:T(8,128)S(1)} %get-tuple-element.10), channel_id=1, source_target_pairs={{0,1},{1,0},{2,3},{3,2},{4,5},{5,4},{6,7},{7,6},{8,9},{9,8},{10,11... | collective-permute-start | bytes 245768 | tf_op jit(solution)/shard_map/ppermute | solution.py:240
  5.8 1.0 %own_gram.1 = f32[80,128]{1,0:T(8,128)S(1)} custom-call(bf16[96,16384]{1,0:T(8,128)(2,1)S(1)} %get-tuple-element.8.right, bf16[1,16384]{1,0:T(2,128)(2,1)S(1)} %get-tuple-element.9.own), custom_call_target="tpu_custom_call" | custom-call | flops 335544320 | bytes 3145728 | tf_op jit(solution)/shard_map/own_gram/pallas_call | solution.py:105
  6.7 0.1 collective-permute-start
  6.8 0.0 collective-permute-done.2
  6.9 2.9 %collective-permute-start.4 = (f32[80,128]{1,0:T(8,128)S(1)}, f32[80,128]{1,0:T(8,128)S(1)}, u32[]{:S(2)}, u32[]{:S(2)}) collective-permute-start(f32[80,128]{1,0:T(8,128)S(1)} %get-tuple-element.11), channel_id=1, source_target_pairs={{0,4},{1,7},{2,6},{3,5},{4,0},{5,3},{6,2},{7,1},{8,12},{9,15},{10,... | collective-permute-start | bytes 122888 | tf_op jit(solution)/shard_map/ppermute | solution.py:243
  9.8 5.7 %collective-permute-start.3 = (f32[80,128]{1,0:T(8,128)S(1)}, f32[80,128]{1,0:T(8,128)S(1)}, u32[]{:S(2)}, u32[]{:S(2)}) collective-permute-start(f32[80,128]{1,0:T(8,128)S(1)} %get-tuple-element.12), channel_id=1, source_target_pairs={{0,124},{1,127},{2,126},{3,125},{4,8},{5,11},{6,10},{7,9},{8,4},{9... | collective-permute-start | bytes 122888 | tf_op jit(solution)/shard_map/ppermute | solution.py:242
  15.5 0.0 collective-permute-done
  15.5 1.6 %collective-permute-start.1 = (f32[80,128]{1,0:T(8,128)S(1)}, f32[80,128]{1,0:T(8,128)S(1)}, u32[]{:S(2)}, u32[]{:S(2)}) collective-permute-start(f32[80,128]{1,0:T(8,128)S(1)} %add.14.own), channel_id=1, source_target_pairs={{0,2},{1,3},{2,0},{3,1},{4,6},{5,7},{6,4},{7,5},{8,10},{9,11},{10,... | collective-permute-start | bytes 122888 | tf_op jit(solution)/shard_map/ppermute | solution.py:245
  17.2 0.0 collective-permute-done.4
  17.2 1.1 %collective-permute-done.3 = f32[80,128]{1,0:T(8,128)S(1)} collective-permute-done((f32[80,128]{1,0:T(8,128)S(1)}, f32[80,128]{1,0:T(8,128)S(1)}, u32[]{:S(2)}, u32[]{:S(2)}) %collective-permute-start.3) | collective-permute-done | bytes 40992 | tf_op jit(solution)/shard_map/ppermute | solution.py:242
  18.3 0.3 collective-permute-start.5
  18.6 2.0 %collective-permute-done.1.high = f32[80,128]{1,0:T(8,128)S(1)} collective-permute-done((f32[80,128]{1,0:T(8,128)S(1)}, f32[80,128]{1,0:T(8,128)S(1)}, u32[]{:S(2)}, u32[]{:S(2)}) %collective-permute-start.1) | collective-permute-done | bytes 40992 | tf_op jit(solution)/shard_map/ppermute | solution.py:245
  20.6 0.0 collective-permute-done.5.theirs
  20.6 6.3 %analysis.1 = bf16[80,32768]{1,0:T(8,128)(2,1)} custom-call(f32[80,128]{1,0:T(8,128)S(1)} %add.14.own, f32[80,128]{1,0:T(8,128)S(1)} %collective-permute-done.1.high, f32[80,128]{1,0:T(8,128)S(1)} %add.16.mine, f32[80,128]{1,0:T(8,128)S(1)} %collective-permute-done.5.theirs, bf16[80,32768]{1,0:T(8,128)(2,1)} %ensemble.1), custom_call_target="tpu_custom_call" | custom-call | tf_op jit(solution)/shard_map/analysis/pallas_call | solution.py:203
  (4 shorter events, 0.0 us)
Async XLA Ops:
  4.3 2.6 %collective-permute-start.2 = (f32[160,128]{1,0:T(8,128)S(1)}, f32[160,128]{1,0:T(8,128)S(1)}, u32[]{:S(2)}, u32[]{:S(2)}) collective-permute-start(f32[160,128]{1,0:T(8,128)S(1)} %get-tuple-element.10), channel_id=1, source_target_pairs={{0,1},{1,0},{2,3},{3,2},{4,5},{5,4},{6,7},{7,6},{8,9},{9,8},{10,11... | collective-permute-start | bytes 245768 | tf_op jit(solution)/shard_map/ppermute | solution.py:240
  6.7 8.8 %collective-permute-start = (f32[80,128]{1,0:T(8,128)S(1)}, f32[80,128]{1,0:T(8,128)S(1)}, u32[]{:S(2)}, u32[]{:S(2)}) collective-permute-start(f32[80,128]{1,0:T(8,128)S(1)} %own_gram.1), channel_id=1, source_target_pairs={{0,1},{1,0},{2,3},{3,2},{4,5},{5,4},{6,7},{7,6},{8,9},{9,8},{10,11... | collective-permute-start | bytes 122888 | tf_op jit(solution)/shard_map/ppermute | solution.py:241
  6.9 10.3 %collective-permute-start.4 = (f32[80,128]{1,0:T(8,128)S(1)}, f32[80,128]{1,0:T(8,128)S(1)}, u32[]{:S(2)}, u32[]{:S(2)}) collective-permute-start(f32[80,128]{1,0:T(8,128)S(1)} %get-tuple-element.11), channel_id=1, source_target_pairs={{0,4},{1,7},{2,6},{3,5},{4,0},{5,3},{6,2},{7,1},{8,12},{9,15},{10,... | collective-permute-start | bytes 122888 | tf_op jit(solution)/shard_map/ppermute | solution.py:243
  9.8 8.5 %collective-permute-start.3 = (f32[80,128]{1,0:T(8,128)S(1)}, f32[80,128]{1,0:T(8,128)S(1)}, u32[]{:S(2)}, u32[]{:S(2)}) collective-permute-start(f32[80,128]{1,0:T(8,128)S(1)} %get-tuple-element.12), channel_id=1, source_target_pairs={{0,124},{1,127},{2,126},{3,125},{4,8},{5,11},{6,10},{7,9},{8,4},{9... | collective-permute-start | bytes 122888 | tf_op jit(solution)/shard_map/ppermute | solution.py:242
  15.5 5.0 %collective-permute-start.1 = (f32[80,128]{1,0:T(8,128)S(1)}, f32[80,128]{1,0:T(8,128)S(1)}, u32[]{:S(2)}, u32[]{:S(2)}) collective-permute-start(f32[80,128]{1,0:T(8,128)S(1)} %add.14.own), channel_id=1, source_target_pairs={{0,2},{1,3},{2,0},{3,1},{4,6},{5,7},{6,4},{7,5},{8,10},{9,11},{10,... | collective-permute-start | bytes 122888 | tf_op jit(solution)/shard_map/ppermute | solution.py:245
  18.3 2.2 %collective-permute-start.5 = (f32[80,128]{1,0:T(8,128)S(1)}, f32[80,128]{1,0:T(8,128)S(1)}, u32[]{:S(2)}, u32[]{:S(2)}) collective-permute-start(f32[80,128]{1,0:T(8,128)S(1)} %add.16.mine), channel_id=1, source_target_pairs={{0,1},{1,0},{2,3},{3,2},{4,5},{5,4},{6,7},{7,6},{8,9},{9,8},{10,11... | collective-permute-start | bytes 122888 | tf_op jit(solution)/shard_map/ppermute | solution.py:246

commit v4 on v3

--- a/solution.py
+++ b/solution.py
@@ -9,10 +9,10 @@
 from jax.sharding import PartitionSpec as P
 
 NS_STEPS = 10
-OBS_CHUNKS = 2
+OBS_CHUNKS = (16384,)
 SIDE_ROWS = 16
 FETCHES = 4
-STORES = (2048, 2048, 4096, 8192, 8192, 4096, 2048, 2048)
+STORES = 16
 VMEM_BYTES = 40 * 1024 * 1024
 
 
@@ -33,28 +33,28 @@
 
 
 def outer_kernel(
-    count, place, pert, innov, rinv, loc, out, right, own, innov_in, rinv_in, loc_in, pert_sem, sem
+    count, pert, innov, rinv, loc, before_out, after_out, right, own, innov_in, rinv_in, loc_in, pert_sem, sem
 ):
     members, width = pert.shape
-    chunk = width // OBS_CHUNKS
+    assert sum(OBS_CHUNKS) == width
+    parts = [(sum(OBS_CHUNKS[:i]), length) for i, length in enumerate(OBS_CHUNKS)]
     sides = [
         pltpu.make_async_copy(source, target, sem.at[i])
         for i, (source, target) in enumerate(((rinv, rinv_in), (loc, loc_in), (innov, innov_in)))
     ]
     blocks = []
-    for i in range(OBS_CHUNKS):
-        part = pl.ds(i * chunk, chunk)
+    for i, (start, length) in enumerate(parts):
+        part = pl.ds(start, length)
         target = right.at[pl.ds(0, members), part]
         blocks.append(pltpu.make_async_copy(pert.at[:, part], target, pert_sem.at[i]))
     for copy in sides + blocks:
         copy.start()
     for copy in sides:
         copy.wait()
-    even = place[0] == 0
     total = None
-    for i in range(OBS_CHUNKS):
-        part = pl.ds(i * chunk, chunk)
-        slots = i * chunk + lax.broadcasted_iota(jnp.int32, (1, chunk), 1)
+    for copy, (start, length) in zip(blocks, parts):
+        part = pl.ds(start, length)
+        slots = start + lax.broadcasted_iota(jnp.int32, (1, length), 1)
         live = (slots < count[0]).astype(jnp.float32)
         scaled = rinv_in[:, part]
         before, mid, after = [
@@ -62,24 +62,26 @@
         ]
         own[:, part] = mid
         right[members:, part] = jnp.broadcast_to(
-            innov_in[:, part].astype(jnp.bfloat16), (SIDE_ROWS, chunk)
+            innov_in[:, part].astype(jnp.bfloat16), (SIDE_ROWS, length)
         )
-        rows = (jnp.where(even, before, after), jnp.where(even, after, before))
-        blocks[i].wait()
+        rows = (before, after)
+        copy.wait()
         gram = weighted_grams(rows, right[:, part])
         total = gram if total is None else total + gram
-    out[...] = widened(total)
-
-
-def outer_grams(pert, innov, rinv, loc, count, place):
+    before_out[...] = widened(total[:members])
+    after_out[...] = widened(total[members:])
+
+
+def outer_grams(pert, innov, rinv, loc, count):
     members, width = pert.shape
     return pl.pallas_call(
         outer_kernel,
-        in_specs=[pl.BlockSpec(memory_space=pltpu.SMEM)] * 2
+        in_specs=[pl.BlockSpec(memory_space=pltpu.SMEM)]
         + [pl.BlockSpec(memory_space=pltpu.HBM)] * 4,
-        out_specs=[pl.BlockSpec(memory_space=pltpu.VMEM)] * 3,
+        out_specs=[pl.BlockSpec(memory_space=pltpu.VMEM)] * 4,
         out_shape=[
-            jax.ShapeDtypeStruct((2 * members, 128), jnp.float32),
+            jax.ShapeDtypeStruct((members, 128), jnp.float32),
+            jax.ShapeDtypeStruct((members, 128), jnp.float32),
             jax.ShapeDtypeStruct((members + SIDE_ROWS, width), jnp.bfloat16),
             jax.ShapeDtypeStruct((1, width), jnp.bfloat16),
         ],
@@ -87,12 +89,12 @@
             pltpu.VMEM((1, width), jnp.float32),
             pltpu.VMEM((1, width), jnp.float32),
             pltpu.VMEM((3, width), jnp.float32),
-            pltpu.SemaphoreType.DMA((OBS_CHUNKS,)),
+            pltpu.SemaphoreType.DMA((len(OBS_CHUNKS),)),
             pltpu.SemaphoreType.DMA((3,)),
         ],
         compiler_params=pltpu.CompilerParams(vmem_limit_bytes=VMEM_BYTES),
         name="outer_grams",
-    )(count, place, *(in_hbm(x) for x in (pert, innov, rinv, loc)))
+    )(count, *(in_hbm(x) for x in (pert, innov, rinv, loc)))
 
 
 def own_kernel(right, own, out):
@@ -162,36 +164,30 @@
         root * inverse_root[:, members : members + 1], axis=0, keepdims=True
     )
     scaled = root * (math.sqrt(members - 1.0) * jnp.sqrt(inv))
-    transform = (scaled + mean_weight).astype(jnp.bfloat16).astype(jnp.float32)[:, :members]
-    keep = 1.0 - jnp.sum(transform, axis=1, keepdims=True)
-    return transform + keep / members
-
-
-def analysis_kernel(own, high, mine, theirs, ensemble, out, held, result, in_sem, out_sem):
+    return (scaled + mean_weight).astype(jnp.bfloat16)[:, :members]
+
+
+def analysis_kernel(mine, theirs, ensemble, out, held, result, in_sem, out_sem):
     members, width = held.shape
-    chunk = width // FETCHES
     fetches, stores, parts = [], [], []
     for i in range(FETCHES):
-        part = pl.ds(i * chunk, chunk)
+        part = pl.ds(i * (width // FETCHES), width // FETCHES)
         fetches.append(pltpu.make_async_copy(ensemble.at[:, part], held.at[:, part], in_sem.at[i]))
-    for i, length in enumerate(STORES):
-        part = pl.ds(sum(STORES[:i]), length)
+    for i in range(STORES):
+        part = pl.ds(i * (width // STORES), width // STORES)
         parts.append(part)
         stores.append(pltpu.make_async_copy(result.at[:, part], out.at[:, part], out_sem.at[i]))
     for copy in fetches:
         copy.start()
-    weights = transform_of((own[...] + high[...]) + (mine[...] + theirs[...]))
-    high = weights.astype(jnp.bfloat16)
-    low = (weights - high.astype(jnp.float32)).astype(jnp.bfloat16)
-    left = jnp.concatenate([high, low], axis=1)
+    transform = transform_of(mine[...] + theirs[...])
+    share = (1.0 - jnp.sum(transform.astype(jnp.float32), axis=1, keepdims=True)) / members
+    left = jnp.concatenate([transform, jnp.ones((SIDE_ROWS, members), jnp.bfloat16)], axis=0)
     for copy in fetches:
         copy.wait()
     for part, copy in zip(parts, stores):
-        block = held[:, part]
-        both = jnp.concatenate([block, block], axis=0)
-        result[:, part] = jnp.dot(left, both, preferred_element_type=jnp.float32).astype(
-            jnp.bfloat16
-        )
+        sums = dot(left, held[:, part])
+        mean = share * sums[members : members + 1]
+        result[:, part] = (sums[:members] + mean).astype(jnp.bfloat16)
         copy.start()
     for copy in stores:
         copy.wait()
@@ -199,7 +195,6 @@
 
 def analysis(grams, ensemble):
     members, width = ensemble.shape
-    assert sum(STORES) == width
     return pl.pallas_call(
         analysis_kernel,
         in_specs=[pl.BlockSpec(memory_space=pltpu.VMEM)] * len(grams) + [pl.BlockSpec(memory_space=pltpu.HBM)],
@@ -209,7 +204,7 @@
             pltpu.VMEM((members, width), jnp.bfloat16),
             pltpu.VMEM((members, width), jnp.bfloat16),
             pltpu.SemaphoreType.DMA((FETCHES,)),
-            pltpu.SemaphoreType.DMA((len(STORES),)),
+            pltpu.SemaphoreType.DMA((STORES,)),
         ],
         compiler_params=pltpu.CompilerParams(vmem_limit_bytes=VMEM_BYTES),
         name="analysis",
@@ -229,21 +224,20 @@
 
     core = pairs(lambda t, l: (t, l ^ 1))
     high = pairs(lambda t, l: (t, l ^ 2))
-    near = pairs(lambda t, l: (t ^ 1, l ^ (2 * (l & 1))))
-    far = pairs(lambda t, l: ((t + 1 if t & 1 else t - 1) % n_tile, l ^ (2 * (l & 1))))
-    place = (lax.axis_index("tile") % 2).astype(jnp.int32)
-    outer, right, weight = outer_grams(
-        obs_pert, innovation[None, :], obs_rinv[None, :], loc_weight, obs_count, place[None]
+    onward = pairs(lambda t, l: ((t + 1) % n_tile, l ^ (2 * (l & 1))))
+    back = pairs(lambda t, l: ((t - 1) % n_tile, l ^ (2 * (l & 1))))
+    before, after, right, weight = outer_grams(
+        obs_pert, innovation[None, :], obs_rinv[None, :], loc_weight, obs_count
     )
     own = own_gram(right, weight)
-    members = own.shape[0]
-    outer = outer + lax.ppermute(outer, axes, core)
-    own = own + lax.ppermute(own, axes, core)
-    from_far = lax.ppermute(outer[:members], axes, far)
-    from_near = lax.ppermute(outer[members:], axes, near)
-    mine = from_far + from_near
+    after = after + lax.ppermute(after, axes, core)
+    before = before + lax.ppermute(before, axes, core)
+    after, own = lax.optimization_barrier((after, own))
+    from_before = lax.ppermute(after, axes, onward)
+    from_after = lax.ppermute(before, axes, back)
     from_high = lax.ppermute(own, axes, high)
-    return analysis((own, from_high, mine, lax.ppermute(mine, axes, core)), ensemble)
+    mine = (own + from_high) + from_after + from_before
+    return analysis((mine, lax.ppermute(mine, axes, core)), ensemble)
 
 
 def solution(mesh):

time: 27 us -> 25.9 us (0.959)
  waiting for transfers between devices: 3.14 us -> 1.98 us
  starting transfers between devices: 12.2 us -> 12.5 us
    ppermute x1, waiting for transfers between devices: 1.98 us -> 0.01 us  [local(): from_high = lax.ppermute(own, axes, high)]
    ppermute x5, starting transfers between devices: 10.5 us -> 12.2 us  [the longest x1 6.43 us: local(): from_after = lax.ppermute(before, axes, back)]
    ppermute x1, starting transfers between devices: 1.63 us -> 0.36 us  [local(): from_high = lax.ppermute(own, axes, high)]
    ppermute x5, waiting for transfers between devices: 1.16 us -> 1.97 us  [the longest x1 0.87 us: local(): return analysis((mine, lax.ppermute(mine, axes, core)), ensemble)]
  transfers between devices with their start and end apart: 6 -> 6, of which waited for: 2 -> 3; matrix products, arithmetic and copies ran while one was open for 0% -> 0% of each run, Pallas kernels for 4% -> 4%
where the time goes in v4:
time: 25.9 us; the launch traced here: 25.8 us
  starting transfers between devices  12.5 us (48%)
  Pallas kernels  10.6 us (41%)
  waiting for transfers between devices  1.98 us (8%)
  between operations  0.69 us (3%)
    ppermute x1, starting transfers between devices, local(): from_after = lax.ppermute(before, axes, back)  6.43 us
    pallas_call x1, Pallas kernels, analysis(): pl.pallas_call(analysis_kernel, in_specs=[pl.BlockSpec(memory_space=pltpu...  6.16 us
    pallas_call x1, Pallas kernels, outer_grams(): pl.pallas_call(outer_kernel, in_specs=[pl.BlockSpec(memory_space=pltpu.SM...  3.45 us
    ppermute x1, starting transfers between devices, local(): from_before = lax.ppermute(after, axes, onward)  2.88 us
    ppermute x1, starting transfers between devices, local(): after = after + lax.ppermute(after, axes, core)  1.5 us
    ppermute x1, starting transfers between devices, local(): return analysis((mine, lax.ppermute(mine, axes, core)), ensemble)  1.25 us
    pallas_call x1, Pallas kernels, own_gram(): pl.pallas_call(own_kernel, in_specs=[pl.BlockSpec(memory_space=pltpu.VMEM...  0.96 us
    ppermute x1, waiting for transfers between devices, local(): return analysis((mine, lax.ppermute(mine, axes, core)), ensemble)  0.87 us
  transfers between devices with their start and end apart: 6, of which 3 were waited for; matrix products, arithmetic and copies ran while one was open for 0% of the time, Pallas kernels for 4%

profile of v4, /device:TPU:1, one launch (start us, length us, event | category | flops | bytes accessed | tf_op | source)
XLA Modules:
  0.0 25.8 jit_solution(279247678223362614)
XLA Ops:
  0.7 3.4 %outer_grams.1 = (f32[80,128]{1,0:T(8,128)S(1)}, f32[80,128]{1,0:T(8,128)S(1)}, bf16[96,16384]{1,0:T(8,128)(2,1)S(1)}, bf16[1,16384]{1,0:T(2,128)(2,1)S(1)}) custom-call(s32[1]{0:T(128)S(6)} %copy.7.count, bf16[80,16384]{1,0:T(8,128)(2,1)} %pert.1, f32[1,16384]{1,0:T(1,128)} %bitcast.2, f32[1,16384]{1,0:T(1,128)} %bitcast.3, f32[3,16384]{1,0:T(4,128)} %loc.1), custom_call_target="tpu_custom_call" | custom-call | tf_op jit(solution)/shard_map/outer_grams/pallas_call | solution.py:77
  4.1 1.5 %collective-permute-start = (f32[80,128]{1,0:T(8,128)S(1)}, f32[80,128]{1,0:T(8,128)S(1)}, u32[]{:S(2)}, u32[]{:S(2)}) collective-permute-start(f32[80,128]{1,0:T(8,128)S(1)} %get-tuple-element.11), channel_id=1, source_target_pairs={{0,1},{1,0},{2,3},{3,2},{4,5},{5,4},{6,7},{7,6},{8,9},{9,8},{10,11... | collective-permute-start | bytes 122888 | tf_op jit(solution)/shard_map/ppermute | solution.py:233
  5.6 0.1 collective-permute-start.2
  5.7 1.0 %own_gram.1 = f32[80,128]{1,0:T(8,128)S(1)} custom-call(bf16[96,16384]{1,0:T(8,128)(2,1)S(1)} %get-tuple-element.12.right, bf16[1,16384]{1,0:T(2,128)(2,1)S(1)} %get-tuple-element.13.own), custom_call_target="tpu_custom_call" | custom-call | flops 335544320 | bytes 3145728 | tf_op jit(solution)/shard_map/own_gram/pallas_call | solution.py:107
  6.7 0.0 collective-permute-done
  6.7 2.9 %collective-permute-start.4 = (f32[80,128]{1,0:T(8,128)S(1)}, f32[80,128]{1,0:T(8,128)S(1)}, u32[]{:S(2)}, u32[]{:S(2)}) collective-permute-start(f32[80,128]{1,0:T(8,128)S(1)} %add.15), channel_id=1, source_target_pairs={{0,4},{1,7},{2,6},{3,5},{4,8},{5,11},{6,10},{7,9},{8,12},{9,15},{1... | collective-permute-start | bytes 122888 | tf_op jit(solution)/shard_map/ppermute | solution.py:236
  9.6 0.4 %collective-permute-start.1 = (f32[80,128]{1,0:T(8,128)S(1)}, f32[80,128]{1,0:T(8,128)S(1)}, u32[]{:S(2)}, u32[]{:S(2)}) collective-permute-start(f32[80,128]{1,0:T(8,128)S(1)} %own_gram.1), channel_id=1, source_target_pairs={{0,2},{1,3},{2,0},{3,1},{4,6},{5,7},{6,4},{7,5},{8,10},{9,11},{10,... | collective-permute-start | bytes 122888 | tf_op jit(solution)/shard_map/ppermute | solution.py:238
  9.9 0.0 collective-permute-done.2
  10.0 6.4 %collective-permute-start.3 = (f32[80,128]{1,0:T(8,128)S(1)}, f32[80,128]{1,0:T(8,128)S(1)}, u32[]{:S(2)}, u32[]{:S(2)}) collective-permute-start(f32[80,128]{1,0:T(8,128)S(1)} %add.17), channel_id=1, source_target_pairs={{0,124},{1,127},{2,126},{3,125},{4,0},{5,3},{6,2},{7,1},{8,4},{9,7... | collective-permute-start | bytes 122888 | tf_op jit(solution)/shard_map/ppermute | solution.py:237
  16.4 0.3 %collective-permute-done.4 = f32[80,128]{1,0:T(8,128)S(1)} collective-permute-done((f32[80,128]{1,0:T(8,128)S(1)}, f32[80,128]{1,0:T(8,128)S(1)}, u32[]{:S(2)}, u32[]{:S(2)}) %collective-permute-start.4) | collective-permute-done | bytes 40992 | tf_op jit(solution)/shard_map/ppermute | solution.py:236
  16.6 0.0 collective-permute-done.1
  16.7 0.8 %collective-permute-done.3 = f32[80,128]{1,0:T(8,128)S(1)} collective-permute-done((f32[80,128]{1,0:T(8,128)S(1)}, f32[80,128]{1,0:T(8,128)S(1)}, u32[]{:S(2)}, u32[]{:S(2)}) %collective-permute-start.3) | collective-permute-done | bytes 40992 | tf_op jit(solution)/shard_map/ppermute | solution.py:237
  17.5 1.2 %collective-permute-start.5 = (f32[80,128]{1,0:T(8,128)S(1)}, f32[80,128]{1,0:T(8,128)S(1)}, u32[]{:S(2)}, u32[]{:S(2)}) collective-permute-start(f32[80,128]{1,0:T(8,128)S(1)} %add_add_fusion.mine), channel_id=1, source_target_pairs={{0,1},{1,0},{2,3},{3,2},{4,5},{5,4},{6,7},{7,6},{8,9},{9,8},{10,11... | collective-permute-start | bytes 122888 | tf_op jit(solution)/shard_map/ppermute | solution.py:240
  18.7 0.9 %collective-permute-done.5.theirs = f32[80,128]{1,0:T(8,128)S(1)} collective-permute-done((f32[80,128]{1,0:T(8,128)S(1)}, f32[80,128]{1,0:T(8,128)S(1)}, u32[]{:S(2)}, u32[]{:S(2)}) %collective-permute-start.5) | collective-permute-done | bytes 40992 | tf_op jit(solution)/shard_map/ppermute | solution.py:240
  19.6 6.2 %analysis.1 = bf16[80,32768]{1,0:T(8,128)(2,1)} custom-call(f32[80,128]{1,0:T(8,128)S(1)} %add_add_fusion.mine, f32[80,128]{1,0:T(8,128)S(1)} %collective-permute-done.5.theirs, bf16[80,32768]{1,0:T(8,128)(2,1)} %ensemble.1), custom_call_target="tpu_custom_call" | custom-call | tf_op jit(solution)/shard_map/analysis/pallas_call | solution.py:198
  (3 shorter events, 0.0 us)
Async XLA Ops:
  4.1 2.6 %collective-permute-start = (f32[80,128]{1,0:T(8,128)S(1)}, f32[80,128]{1,0:T(8,128)S(1)}, u32[]{:S(2)}, u32[]{:S(2)}) collective-permute-start(f32[80,128]{1,0:T(8,128)S(1)} %get-tuple-element.11), channel_id=1, source_target_pairs={{0,1},{1,0},{2,3},{3,2},{4,5},{5,4},{6,7},{7,6},{8,9},{9,8},{10,11... | collective-permute-start | bytes 122888 | tf_op jit(solution)/shard_map/ppermute | solution.py:233
  5.6 4.3 %collective-permute-start.2 = (f32[80,128]{1,0:T(8,128)S(1)}, f32[80,128]{1,0:T(8,128)S(1)}, u32[]{:S(2)}, u32[]{:S(2)}) collective-permute-start(f32[80,128]{1,0:T(8,128)S(1)} %get-tuple-element.15), channel_id=1, source_target_pairs={{0,1},{1,0},{2,3},{3,2},{4,5},{5,4},{6,7},{7,6},{8,9},{9,8},{10,11... | collective-permute-start | bytes 122888 | tf_op jit(solution)/shard_map/ppermute | solution.py:234
  6.7 9.9 %collective-permute-start.4 = (f32[80,128]{1,0:T(8,128)S(1)}, f32[80,128]{1,0:T(8,128)S(1)}, u32[]{:S(2)}, u32[]{:S(2)}) collective-permute-start(f32[80,128]{1,0:T(8,128)S(1)} %add.15), channel_id=1, source_target_pairs={{0,4},{1,7},{2,6},{3,5},{4,8},{5,11},{6,10},{7,9},{8,12},{9,15},{1... | collective-permute-start | bytes 122888 | tf_op jit(solution)/shard_map/ppermute | solution.py:236
  9.6 7.1 %collective-permute-start.1 = (f32[80,128]{1,0:T(8,128)S(1)}, f32[80,128]{1,0:T(8,128)S(1)}, u32[]{:S(2)}, u32[]{:S(2)}) collective-permute-start(f32[80,128]{1,0:T(8,128)S(1)} %own_gram.1), channel_id=1, source_target_pairs={{0,2},{1,3},{2,0},{3,1},{4,6},{5,7},{6,4},{7,5},{8,10},{9,11},{10,... | collective-permute-start | bytes 122888 | tf_op jit(solution)/shard_map/ppermute | solution.py:238
  10.0 7.5 %collective-permute-start.3 = (f32[80,128]{1,0:T(8,128)S(1)}, f32[80,128]{1,0:T(8,128)S(1)}, u32[]{:S(2)}, u32[]{:S(2)}) collective-permute-start(f32[80,128]{1,0:T(8,128)S(1)} %add.17), channel_id=1, source_target_pairs={{0,124},{1,127},{2,126},{3,125},{4,0},{5,3},{6,2},{7,1},{8,4},{9,7... | collective-permute-start | bytes 122888 | tf_op jit(solution)/shard_map/ppermute | solution.py:237
  17.5 2.1 %collective-permute-start.5 = (f32[80,128]{1,0:T(8,128)S(1)}, f32[80,128]{1,0:T(8,128)S(1)}, u32[]{:S(2)}, u32[]{:S(2)}) collective-permute-start(f32[80,128]{1,0:T(8,128)S(1)} %add_add_fusion.mine), channel_id=1, source_target_pairs={{0,1},{1,0},{2,3},{3,2},{4,5},{5,4},{6,7},{7,6},{8,9},{9,8},{10,11... | collective-permute-start | bytes 122888 | tf_op jit(solution)/shard_map/ppermute | solution.py:240

commit v5 on v4

--- a/solution.py
+++ b/solution.py
@@ -33,7 +33,7 @@
 
 
 def outer_kernel(
-    count, pert, innov, rinv, loc, before_out, after_out, right, own, innov_in, rinv_in, loc_in, pert_sem, sem
+    count, pert, innov, rinv, loc, out, right, own, innov_in, rinv_in, loc_in, pert_sem, sem
 ):
     members, width = pert.shape
     assert sum(OBS_CHUNKS) == width
@@ -68,8 +68,7 @@
         copy.wait()
         gram = weighted_grams(rows, right[:, part])
         total = gram if total is None else total + gram
-    before_out[...] = widened(total[:members])
-    after_out[...] = widened(total[members:])
+    out[...] = widened(total)
 
 
 def outer_grams(pert, innov, rinv, loc, count):
@@ -78,10 +77,9 @@
         outer_kernel,
         in_specs=[pl.BlockSpec(memory_space=pltpu.SMEM)]
         + [pl.BlockSpec(memory_space=pltpu.HBM)] * 4,
-        out_specs=[pl.BlockSpec(memory_space=pltpu.VMEM)] * 4,
+        out_specs=[pl.BlockSpec(memory_space=pltpu.VMEM)] * 3,
         out_shape=[
-            jax.ShapeDtypeStruct((members, 128), jnp.float32),
-            jax.ShapeDtypeStruct((members, 128), jnp.float32),
+            jax.ShapeDtypeStruct((2 * members, 128), jnp.float32),
             jax.ShapeDtypeStruct((members + SIDE_ROWS, width), jnp.bfloat16),
             jax.ShapeDtypeStruct((1, width), jnp.bfloat16),
         ],
@@ -144,21 +142,31 @@
     cols = lax.broadcasted_iota(jnp.int32, total.shape, 1)
     eye = (rows == cols).astype(jnp.float32)
     square = cols < members
-    wide = jnp.where(cols <= members, total, 0.0) + (members - 1.0) * eye
-    mat = jnp.where(square, wide, 0.0)
-    proj = wide - mat
-    parts = split(wide)
-    squared = product(parts, parts)
+    mat = jnp.where(square, total, 0.0) + (members - 1.0) * eye
+    proj = jnp.where(cols == members, total, 0.0)
+    mat_parts = split(mat)
+    squared = product(mat_parts, mat_parts)
     inv = 1.0 / jnp.sqrt(jnp.sum(mat * mat, keepdims=True))
-    head = jnp.where(square, squared, 0.0)
-    iterate = split((1.5 * inv) * mat - (0.5 * inv * inv) * head)
-    inverse_root = 1.5 * (eye + proj) - (0.5 * inv) * (mat + (squared - head))
-    for step in range(1, NS_STEPS):
-        root_parts = split(inverse_root)
-        factor = split(1.5 * eye - 0.5 * product(root_parts, iterate))
-        if step < NS_STEPS - 1:
-            iterate = split(product(iterate, factor))
-        inverse_root = product(factor, root_parts)
+    first = mat * inv
+    second = squared * (inv * inv)
+    inverse_root = eye + proj
+    for triple in range((NS_STEPS - 1) // 3):
+        first_parts = split(first)
+        if triple:
+            second = product(first_parts, first_parts)
+        second_parts = split(second)
+        third = product(second_parts, first_parts)
+        fourth = product(second_parts, second_parts)
+        pair = 2.25 * eye - 2.4375 * first + 1.6875 * second - 0.5625 * third + 0.0625 * fourth
+        pair_parts = split(pair)
+        pair_squared = split(product(pair_parts, pair_parts))
+        first_pair = product(first_parts, pair_parts)
+        second_pair = split(product(second_parts, pair_parts))
+        factor = split(1.5 * pair - 0.5 * product(pair_squared, split(first_pair)))
+        scaled = split(1.5 * first_pair - 0.5 * product(second_pair, pair_squared))
+        first = product(scaled, factor)
+        inverse_root = product(factor, split(inverse_root))
+    inverse_root = product(split(1.5 * eye - 0.5 * first), split(inverse_root))
     root = jnp.where(square, inverse_root, 0.0)
     mean_weight = inv * jnp.sum(
         root * inverse_root[:, members : members + 1], axis=0, keepdims=True
@@ -226,17 +234,18 @@
     high = pairs(lambda t, l: (t, l ^ 2))
     onward = pairs(lambda t, l: ((t + 1) % n_tile, l ^ (2 * (l & 1))))
     back = pairs(lambda t, l: ((t - 1) % n_tile, l ^ (2 * (l & 1))))
-    before, after, right, weight = outer_grams(
+    outer, right, weight = outer_grams(
         obs_pert, innovation[None, :], obs_rinv[None, :], loc_weight, obs_count
     )
     own = own_gram(right, weight)
-    after = after + lax.ppermute(after, axes, core)
-    before = before + lax.ppermute(before, axes, core)
+    members = own.shape[0]
+    outer = outer + lax.ppermute(outer, axes, core)
+    before, after = outer[:members], outer[members:]
     after, own = lax.optimization_barrier((after, own))
     from_before = lax.ppermute(after, axes, onward)
     from_after = lax.ppermute(before, axes, back)
     from_high = lax.ppermute(own, axes, high)
-    mine = (own + from_high) + from_after + from_before
+    mine = from_after + (own + from_high) + from_before
     return analysis((mine, lax.ppermute(mine, axes, core)), ensemble)
 
 

time: 25.9 us -> 25.4 us (0.981)
  starting transfers between devices: 12.5 us -> 12.2 us
  Pallas kernels: 10.6 us -> 10.3 us
    pallas_call x1, Pallas kernels: 6.16 us -> 5.86 us  [analysis(): pl.pallas_call(analysis_kernel, in_specs=[pl.BlockSpec(memory_space=pltpu...]
    ppermute x2 -> x1, starting transfers between devices: 1.6 us -> 1.5 us  [local(): outer = outer + lax.ppermute(outer, axes, core)]
  transfers between devices with their start and end apart: 6 -> 5, of which waited for: 3 -> 3; matrix products, arithmetic and copies ran while one was open for 0% -> 0% of each run, Pallas kernels for 4% -> 4%
where the time goes in v5:
time: 25.4 us; the launch traced here: 25.2 us
  starting transfers between devices  12.2 us (48%)
  Pallas kernels  10.3 us (41%)
  waiting for transfers between devices  1.97 us (8%)
  between operations  0.7 us (3%)
    ppermute x1, starting transfers between devices, local(): from_after = lax.ppermute(before, axes, back)  6.37 us
    pallas_call x1, Pallas kernels, analysis(): pl.pallas_call(analysis_kernel, in_specs=[pl.BlockSpec(memory_space=pltpu...  5.86 us
    pallas_call x1, Pallas kernels, outer_grams(): pl.pallas_call(outer_kernel, in_specs=[pl.BlockSpec(memory_space=pltpu.SM...  3.45 us
    ppermute x1, starting transfers between devices, local(): from_before = lax.ppermute(after, axes, onward)  2.88 us
    ppermute x1, starting transfers between devices, local(): outer = outer + lax.ppermute(outer, axes, core)  1.5 us
    ppermute x1, starting transfers between devices, local(): return analysis((mine, lax.ppermute(mine, axes, core)), ensemble)  1.12 us
    pallas_call x1, Pallas kernels, own_gram(): pl.pallas_call(own_kernel, in_specs=[pl.BlockSpec(memory_space=pltpu.VMEM...  0.96 us
    ppermute x1, waiting for transfers between devices, local(): return analysis((mine, lax.ppermute(mine, axes, core)), ensemble)  0.87 us
  transfers between devices with their start and end apart: 5, of which 3 were waited for; matrix products, arithmetic and copies ran while one was open for 0% of the time, Pallas kernels for 4%

profile of v5, /device:TPU:1, one launch (start us, length us, event | category | flops | bytes accessed | tf_op | source)
XLA Modules:
  0.0 25.2 jit_solution(8023101643855038449)
XLA Ops:
  0.7 3.4 %outer_grams.1 = (f32[160,128]{1,0:T(8,128)S(1)}, bf16[96,16384]{1,0:T(8,128)(2,1)S(1)}, bf16[1,16384]{1,0:T(2,128)(2,1)S(1)}) custom-call(s32[1]{0:T(128)S(6)} %copy.7.count, bf16[80,16384]{1,0:T(8,128)(2,1)} %pert.1, f32[1,16384]{1,0:T(1,128)} %bitcast.2, f32[1,16384]{1,0:T(1,128)} %bitcast.3, f32[3,16384]{1,0:T(4,128)} %loc.1), custom_call_target="tpu_custom_call" | custom-call | tf_op jit(solution)/shard_map/outer_grams/pallas_call | solution.py:76
  4.1 1.5 %collective-permute-start = (f32[160,128]{1,0:T(8,128)S(1)}, f32[160,128]{1,0:T(8,128)S(1)}, u32[]{:S(2)}, u32[]{:S(2)}) collective-permute-start(f32[160,128]{1,0:T(8,128)S(1)} %get-tuple-element.10), channel_id=1, source_target_pairs={{0,1},{1,0},{2,3},{3,2},{4,5},{5,4},{6,7},{7,6},{8,9},{9,8},{10,11... | collective-permute-start | bytes 245768 | tf_op jit(solution)/shard_map/ppermute | solution.py:242
  5.6 1.0 %own_gram.1 = f32[80,128]{1,0:T(8,128)S(1)} custom-call(bf16[96,16384]{1,0:T(8,128)(2,1)S(1)} %get-tuple-element.11.right, bf16[1,16384]{1,0:T(2,128)(2,1)S(1)} %get-tuple-element.12.own), custom_call_target="tpu_custom_call" | custom-call | flops 335544320 | bytes 3145728 | tf_op jit(solution)/shard_map/own_gram/pallas_call | solution.py:105
  6.6 0.0 collective-permute-done
  6.6 2.9 %collective-permute-start.3 = (f32[80,128]{1,0:T(8,128)S(1)}, f32[80,128]{1,0:T(8,128)S(1)}, u32[]{:S(2)}, u32[]{:S(2)}) collective-permute-start(f32[80,128]{1,0:T(8,128)S(1)} %get-tuple-element.14), channel_id=1, source_target_pairs={{0,4},{1,7},{2,6},{3,5},{4,8},{5,11},{6,10},{7,9},{8,12},{9,15},{1... | collective-permute-start | bytes 122888 | tf_op jit(solution)/shard_map/ppermute | solution.py:245
  9.5 0.4 %collective-permute-start.2 = (f32[80,128]{1,0:T(8,128)S(1)}, f32[80,128]{1,0:T(8,128)S(1)}, u32[]{:S(2)}, u32[]{:S(2)}) collective-permute-start(f32[80,128]{1,0:T(8,128)S(1)} %own_gram.1), channel_id=1, source_target_pairs={{0,2},{1,3},{2,0},{3,1},{4,6},{5,7},{6,4},{7,5},{8,10},{9,11},{10,... | collective-permute-start | bytes 122888 | tf_op jit(solution)/shard_map/ppermute | solution.py:247
  9.9 6.4 %collective-permute-start.1 = (f32[80,128]{1,0:T(8,128)S(1)}, f32[80,128]{1,0:T(8,128)S(1)}, u32[]{:S(2)}, u32[]{:S(2)}) collective-permute-start(f32[80,128]{1,0:T(8,128)S(1)} %get-tuple-element.15), channel_id=1, source_target_pairs={{0,124},{1,127},{2,126},{3,125},{4,0},{5,3},{6,2},{7,1},{8,4},{9,7... | collective-permute-start | bytes 122888 | tf_op jit(solution)/shard_map/ppermute | solution.py:246
  16.2 0.4 %collective-permute-done.3 = f32[80,128]{1,0:T(8,128)S(1)} collective-permute-done((f32[80,128]{1,0:T(8,128)S(1)}, f32[80,128]{1,0:T(8,128)S(1)}, u32[]{:S(2)}, u32[]{:S(2)}) %collective-permute-start.3) | collective-permute-done | bytes 40992 | tf_op jit(solution)/shard_map/ppermute | solution.py:245
  16.6 0.0 collective-permute-done.2
  16.6 0.7 %collective-permute-done.1 = f32[80,128]{1,0:T(8,128)S(1)} collective-permute-done((f32[80,128]{1,0:T(8,128)S(1)}, f32[80,128]{1,0:T(8,128)S(1)}, u32[]{:S(2)}, u32[]{:S(2)}) %collective-permute-start.1) | collective-permute-done | bytes 40992 | tf_op jit(solution)/shard_map/ppermute | solution.py:246
  17.3 1.1 %collective-permute-start.4 = (f32[80,128]{1,0:T(8,128)S(1)}, f32[80,128]{1,0:T(8,128)S(1)}, u32[]{:S(2)}, u32[]{:S(2)}) collective-permute-start(f32[80,128]{1,0:T(8,128)S(1)} %add_add_fusion.mine), channel_id=1, source_target_pairs={{0,1},{1,0},{2,3},{3,2},{4,5},{5,4},{6,7},{7,6},{8,9},{9,8},{10,11... | collective-permute-start | bytes 122888 | tf_op jit(solution)/shard_map/ppermute | solution.py:249
  18.5 0.9 %collective-permute-done.4.theirs = f32[80,128]{1,0:T(8,128)S(1)} collective-permute-done((f32[80,128]{1,0:T(8,128)S(1)}, f32[80,128]{1,0:T(8,128)S(1)}, u32[]{:S(2)}, u32[]{:S(2)}) %collective-permute-start.4) | collective-permute-done | bytes 40992 | tf_op jit(solution)/shard_map/ppermute | solution.py:249
  19.3 5.9 %analysis.1 = bf16[80,32768]{1,0:T(8,128)(2,1)} custom-call(f32[80,128]{1,0:T(8,128)S(1)} %add_add_fusion.mine, f32[80,128]{1,0:T(8,128)S(1)} %collective-permute-done.4.theirs, bf16[80,32768]{1,0:T(8,128)(2,1)} %ensemble.1), custom_call_target="tpu_custom_call" | custom-call | tf_op jit(solution)/shard_map/analysis/pallas_call | solution.py:206
  (3 shorter events, 0.0 us)
Async XLA Ops:
  4.1 2.5 %collective-permute-start = (f32[160,128]{1,0:T(8,128)S(1)}, f32[160,128]{1,0:T(8,128)S(1)}, u32[]{:S(2)}, u32[]{:S(2)}) collective-permute-start(f32[160,128]{1,0:T(8,128)S(1)} %get-tuple-element.10), channel_id=1, source_target_pairs={{0,1},{1,0},{2,3},{3,2},{4,5},{5,4},{6,7},{7,6},{8,9},{9,8},{10,11... | collective-permute-start | bytes 245768 | tf_op jit(solution)/shard_map/ppermute | solution.py:242
  6.6 10.0 %collective-permute-start.3 = (f32[80,128]{1,0:T(8,128)S(1)}, f32[80,128]{1,0:T(8,128)S(1)}, u32[]{:S(2)}, u32[]{:S(2)}) collective-permute-start(f32[80,128]{1,0:T(8,128)S(1)} %get-tuple-element.14), channel_id=1, source_target_pairs={{0,4},{1,7},{2,6},{3,5},{4,8},{5,11},{6,10},{7,9},{8,12},{9,15},{1... | collective-permute-start | bytes 122888 | tf_op jit(solution)/shard_map/ppermute | solution.py:245
  9.5 7.1 %collective-permute-start.2 = (f32[80,128]{1,0:T(8,128)S(1)}, f32[80,128]{1,0:T(8,128)S(1)}, u32[]{:S(2)}, u32[]{:S(2)}) collective-permute-start(f32[80,128]{1,0:T(8,128)S(1)} %own_gram.1), channel_id=1, source_target_pairs={{0,2},{1,3},{2,0},{3,1},{4,6},{5,7},{6,4},{7,5},{8,10},{9,11},{10,... | collective-permute-start | bytes 122888 | tf_op jit(solution)/shard_map/ppermute | solution.py:247
  9.9 7.5 %collective-permute-start.1 = (f32[80,128]{1,0:T(8,128)S(1)}, f32[80,128]{1,0:T(8,128)S(1)}, u32[]{:S(2)}, u32[]{:S(2)}) collective-permute-start(f32[80,128]{1,0:T(8,128)S(1)} %get-tuple-element.15), channel_id=1, source_target_pairs={{0,124},{1,127},{2,126},{3,125},{4,0},{5,3},{6,2},{7,1},{8,4},{9,7... | collective-permute-start | bytes 122888 | tf_op jit(solution)/shard_map/ppermute | solution.py:246
  17.3 2.0 %collective-permute-start.4 = (f32[80,128]{1,0:T(8,128)S(1)}, f32[80,128]{1,0:T(8,128)S(1)}, u32[]{:S(2)}, u32[]{:S(2)}) collective-permute-start(f32[80,128]{1,0:T(8,128)S(1)} %add_add_fusion.mine), channel_id=1, source_target_pairs={{0,1},{1,0},{2,3},{3,2},{4,5},{5,4},{6,7},{7,6},{8,9},{9,8},{10,11... | collective-permute-start | bytes 122888 | tf_op jit(solution)/shard_map/ppermute | solution.py:249

commit v6 on v5

--- a/solution.py
+++ b/solution.py
@@ -32,8 +32,8 @@
     )
 
 
-def outer_kernel(
-    count, pert, innov, rinv, loc, out, right, own, innov_in, rinv_in, loc_in, pert_sem, sem
+def next_kernel(
+    count, pert, innov, rinv, loc, out, right, first, second, innov_in, rinv_in, loc_in, pert_sem, sem
 ):
     members, width = pert.shape
     assert sum(OBS_CHUNKS) == width
@@ -60,27 +60,28 @@
         before, mid, after = [
             (scaled * loc_in[j : j + 1, part] * live).astype(jnp.bfloat16) for j in range(3)
         ]
-        own[:, part] = mid
+        first[:, part] = before
+        second[:, part] = mid
         right[members:, part] = jnp.broadcast_to(
             innov_in[:, part].astype(jnp.bfloat16), (SIDE_ROWS, length)
         )
-        rows = (before, after)
-        copy.wait()
-        gram = weighted_grams(rows, right[:, part])
+        copy.wait()
+        gram = weighted_grams((after,), right[:, part])
         total = gram if total is None else total + gram
     out[...] = widened(total)
 
 
-def outer_grams(pert, innov, rinv, loc, count):
+def next_gram(pert, innov, rinv, loc, count):
     members, width = pert.shape
     return pl.pallas_call(
-        outer_kernel,
+        next_kernel,
         in_specs=[pl.BlockSpec(memory_space=pltpu.SMEM)]
         + [pl.BlockSpec(memory_space=pltpu.HBM)] * 4,
-        out_specs=[pl.BlockSpec(memory_space=pltpu.VMEM)] * 3,
+        out_specs=[pl.BlockSpec(memory_space=pltpu.VMEM)] * 4,
         out_shape=[
-            jax.ShapeDtypeStruct((2 * members, 128), jnp.float32),
+            jax.ShapeDtypeStruct((members, 128), jnp.float32),
             jax.ShapeDtypeStruct((members + SIDE_ROWS, width), jnp.bfloat16),
+            jax.ShapeDtypeStruct((1, width), jnp.bfloat16),
             jax.ShapeDtypeStruct((1, width), jnp.bfloat16),
         ],
         scratch_shapes=[
@@ -91,19 +92,19 @@
             pltpu.SemaphoreType.DMA((3,)),
         ],
         compiler_params=pltpu.CompilerParams(vmem_limit_bytes=VMEM_BYTES),
-        name="outer_grams",
+        name="next_gram",
     )(count, *(in_hbm(x) for x in (pert, innov, rinv, loc)))
 
 
-def own_kernel(right, own, out):
+def one_kernel(right, own, out):
     out[...] = widened(weighted_grams((own[...],), right[...]))
 
 
-def own_gram(right, own):
+def one_gram(right, own):
     members = right.shape[0] - SIDE_ROWS
     width = right.shape[1]
     return pl.pallas_call(
-        own_kernel,
+        one_kernel,
         in_specs=[pl.BlockSpec(memory_space=pltpu.VMEM)] * 2,
         out_specs=pl.BlockSpec(memory_space=pltpu.VMEM),
         out_shape=jax.ShapeDtypeStruct((members, 128), jnp.float32),
@@ -111,7 +112,7 @@
         cost_estimate=pl.CostEstimate(
             flops=2 * members * 128 * width, bytes_accessed=2 * right.size, transcendentals=0
         ),
-        name="own_gram",
+        name="one_gram",
     )(right, own)
 
 
@@ -231,21 +232,25 @@
         ]
 
     core = pairs(lambda t, l: (t, l ^ 1))
-    high = pairs(lambda t, l: (t, l ^ 2))
     onward = pairs(lambda t, l: ((t + 1) % n_tile, l ^ (2 * (l & 1))))
     back = pairs(lambda t, l: ((t - 1) % n_tile, l ^ (2 * (l & 1))))
-    outer, right, weight = outer_grams(
+    early = pairs(lambda t, l: (t, l ^ 2 if t % 8 == 0 else l ^ 1))
+    late = pairs(lambda t, l: (t, l ^ 1 if t % 8 == 0 else l ^ 2))
+    after, right, row_before, row_own = next_gram(
         obs_pert, innovation[None, :], obs_rinv[None, :], loc_weight, obs_count
     )
-    own = own_gram(right, weight)
-    members = own.shape[0]
-    outer = outer + lax.ppermute(outer, axes, core)
-    before, after = outer[:members], outer[members:]
-    after, own = lax.optimization_barrier((after, own))
+    before = one_gram(right, row_before)
+    after = after + lax.ppermute(after, axes, core)
+    after, before, row_own = lax.optimization_barrier((after, before, row_own))
+    own = one_gram(right, row_own)
+    before = before + lax.ppermute(before, axes, core)
+    before, held = lax.optimization_barrier((before, own))
     from_before = lax.ppermute(after, axes, onward)
+    from_early = lax.ppermute(own, axes, early)
     from_after = lax.ppermute(before, axes, back)
-    from_high = lax.ppermute(own, axes, high)
-    mine = from_after + (own + from_high) + from_before
+    from_late = lax.ppermute(held, axes, late)
+    first = lax.axis_index("tile") % 8 == 0
+    mine = from_before + jnp.where(first, from_early, 0.0) + from_after + jnp.where(first, 0.0, from_late) + own
     return analysis((mine, lax.ppermute(mine, axes, core)), ensemble)
 
 

time: 25.4 us -> 24.8 us (0.976)
  starting transfers between devices: 12.2 us -> 11 us
  Pallas kernels: 10.3 us -> 10.7 us
  waiting for transfers between devices: 1.97 us -> 2.28 us
    ppermute x1, starting transfers between devices: 1.12 us -> 0.24 us  [local(): return analysis((mine, lax.ppermute(mine, axes, core)), ensemble)]
    ppermute x1, starting transfers between devices: 6.37 us -> 5.72 us  [local(): from_after = lax.ppermute(before, axes, back)]
    ppermute x1, waiting for transfers between devices: 0.41 us -> 0.01 us  [local(): from_before = lax.ppermute(after, axes, onward)]
    ppermute x1, waiting for transfers between devices: 0.68 us -> 1.09 us  [local(): from_after = lax.ppermute(before, axes, back)]
    pallas_call x2 -> x3, Pallas kernels: 4.41 us -> 4.82 us  [the longest x1 2.9 us: next_gram(): pl.pallas_call(next_kernel, in_specs=[pl.BlockSpec(memory_space=pltpu.SME...]
    ppermute x2 -> x4, starting transfers between devices: 1.86 us -> 2.19 us  [the longest x1 1.5 us: local(): after = after + lax.ppermute(after, axes, core)]
  transfers between devices with their start and end apart: 5 -> 7, of which waited for: 3 -> 3; matrix products, arithmetic and copies ran while one was open for 0% -> 0% of each run, Pallas kernels for 4% -> 8%
where the time goes in v6:
time: 24.8 us; the launch traced here: 24.7 us
  starting transfers between devices  11 us (44%)
  Pallas kernels  10.7 us (43%)
  waiting for transfers between devices  2.28 us (9%)
  between operations  0.7 us (3%)
    pallas_call x1, Pallas kernels, analysis(): pl.pallas_call(analysis_kernel, in_specs=[pl.BlockSpec(memory_space=pltpu...  5.86 us
    ppermute x1, starting transfers between devices, local(): from_after = lax.ppermute(before, axes, back)  5.72 us
    pallas_call x1, Pallas kernels, next_gram(): pl.pallas_call(next_kernel, in_specs=[pl.BlockSpec(memory_space=pltpu.SME...  2.9 us
    ppermute x1, starting transfers between devices, local(): from_before = lax.ppermute(after, axes, onward)  2.82 us
    pallas_call x2, Pallas kernels, one_gram(): pl.pallas_call(one_kernel, in_specs=[pl.BlockSpec(memory_space=pltpu.VMEM...  1.91 us
    ppermute x1, starting transfers between devices, local(): after = after + lax.ppermute(after, axes, core)  1.5 us
    ppermute x1, waiting for transfers between devices, local(): from_after = lax.ppermute(before, axes, back)  1.09 us
    ppermute x1, waiting for transfers between devices, local(): return analysis((mine, lax.ppermute(mine, axes, core)), ensemble)  1.06 us
  transfers between devices with their start and end apart: 7, of which 3 were waited for; matrix products, arithmetic and copies ran while one was open for 0% of the time, Pallas kernels for 8%

profile of v6, /device:TPU:1, one launch (start us, length us, event | category | flops | bytes accessed | tf_op | source)
XLA Modules:
  0.0 24.7 jit_solution(5940145259914581253)
XLA Ops:
  0.7 2.9 %next_gram.1 = (f32[80,128]{1,0:T(8,128)S(1)}, bf16[96,16384]{1,0:T(8,128)(2,1)S(1)}, bf16[1,16384]{1,0:T(2,128)(2,1)S(1)}, bf16[1,16384]{1,0:T(2,128)(2,1)S(1)}) custom-call(s32[1]{0:T(128)S(6)} %copy.7.count, bf16[80,16384]{1,0:T(8,128)(2,1)} %pert.1, f32[1,16384]{1,0:T(1,128)} %bitcast.2, f32[1,16384]{1,0:T(1,128)} %bitcast.3, f32[3,16384]{1,0:T(4,128)} %loc.1), custom_call_target="tpu_custom_call" | custom-call | tf_op jit(solution)/shard_map/next_gram/pallas_call | solution.py:76
  3.6 1.5 %collective-permute-start = (f32[80,128]{1,0:T(8,128)S(1)}, f32[80,128]{1,0:T(8,128)S(1)}, u32[]{:S(2)}, u32[]{:S(2)}) collective-permute-start(f32[80,128]{1,0:T(8,128)S(1)} %get-tuple-element.14), channel_id=1, source_target_pairs={{0,1},{1,0},{2,3},{3,2},{4,5},{5,4},{6,7},{7,6},{8,9},{9,8},{10,11... | collective-permute-start | bytes 122888 | tf_op jit(solution)/shard_map/ppermute | solution.py:243
  5.1 1.0 %one_gram.2 = f32[80,128]{1,0:T(8,128)S(1)} custom-call(bf16[96,16384]{1,0:T(8,128)(2,1)S(1)} %get-tuple-element.15.right, bf16[1,16384]{1,0:T(2,128)(2,1)S(1)} %get-tuple-element.16.own), custom_call_target="tpu_custom_call" | custom-call | flops 335544320 | bytes 3145728 | tf_op jit(solution)/shard_map/one_gram/pallas_call | solution.py:106
  6.0 0.0 collective-permute-done
  6.1 0.3 %collective-permute-start.3 = (f32[80,128]{1,0:T(8,128)S(1)}, f32[80,128]{1,0:T(8,128)S(1)}, u32[]{:S(2)}, u32[]{:S(2)}) collective-permute-start(f32[80,128]{1,0:T(8,128)S(1)} %one_gram.2), channel_id=1, source_target_pairs={{0,1},{1,0},{2,3},{3,2},{4,5},{5,4},{6,7},{7,6},{8,9},{9,8},{10,11... | collective-permute-start | bytes 122888 | tf_op jit(solution)/shard_map/ppermute | solution.py:246
  6.3 2.8 %collective-permute-start.1 = (f32[80,128]{1,0:T(8,128)S(1)}, f32[80,128]{1,0:T(8,128)S(1)}, u32[]{:S(2)}, u32[]{:S(2)}) collective-permute-start(f32[80,128]{1,0:T(8,128)S(1)} %add.22), channel_id=1, source_target_pairs={{0,4},{1,7},{2,6},{3,5},{4,8},{5,11},{6,10},{7,9},{8,12},{9,15},{1... | collective-permute-start | bytes 122888 | tf_op jit(solution)/shard_map/ppermute | solution.py:248
  9.1 1.0 %one_gram.3 = f32[80,128]{1,0:T(8,128)S(1)} custom-call(bf16[96,16384]{1,0:T(8,128)(2,1)S(1)} %get-tuple-element.15.right, bf16[1,16384]{1,0:T(2,128)(2,1)S(1)} %get-tuple-element.19.own), custom_call_target="tpu_custom_call" | custom-call | flops 335544320 | bytes 3145728 | tf_op jit(solution)/shard_map/one_gram/pallas_call | solution.py:106
  10.1 0.4 %collective-permute-start.2 = (f32[80,128]{1,0:T(8,128)S(1)}, f32[80,128]{1,0:T(8,128)S(1)}, u32[]{:S(2)}, u32[]{:S(2)}) collective-permute-start(f32[80,128]{1,0:T(8,128)S(1)} %one_gram.3), channel_id=1, source_target_pairs={{0,2},{1,3},{2,0},{3,1},{4,5},{5,4},{6,7},{7,6},{8,9},{9,8},{10,11... | collective-permute-start | bytes 122888 | tf_op jit(solution)/shard_map/ppermute | solution.py:249
  10.5 0.0 collective-permute-done.3
  10.5 5.7 %collective-permute-start.4 = (f32[80,128]{1,0:T(8,128)S(1)}, f32[80,128]{1,0:T(8,128)S(1)}, u32[]{:S(2)}, u32[]{:S(2)}) collective-permute-start(f32[80,128]{1,0:T(8,128)S(1)} %add.25), channel_id=1, source_target_pairs={{0,124},{1,127},{2,126},{3,125},{4,0},{5,3},{6,2},{7,1},{8,4},{9,7... | collective-permute-start | bytes 122888 | tf_op jit(solution)/shard_map/ppermute | solution.py:250
  16.3 0.0 collective-permute-start.5
  16.3 0.0 collective-permute-done.1
  16.3 0.0 collective-permute-done.2
  16.3 1.1 %collective-permute-done.4 = f32[80,128]{1,0:T(8,128)S(1)} collective-permute-done((f32[80,128]{1,0:T(8,128)S(1)}, f32[80,128]{1,0:T(8,128)S(1)}, u32[]{:S(2)}, u32[]{:S(2)}) %collective-permute-start.4) | collective-permute-done | bytes 40992 | tf_op jit(solution)/shard_map/ppermute | solution.py:250
  17.4 0.1 collective-permute-done.5
  17.5 0.2 collective-permute-start.6
  17.7 1.1 %collective-permute-done.6.theirs = f32[80,128]{1,0:T(8,128)S(1)} collective-permute-done((f32[80,128]{1,0:T(8,128)S(1)}, f32[80,128]{1,0:T(8,128)S(1)}, u32[]{:S(2)}, u32[]{:S(2)}) %collective-permute-start.6) | collective-permute-done | bytes 40992 | tf_op jit(solution)/shard_map/ppermute | solution.py:254
  18.8 5.9 %analysis.1 = bf16[80,32768]{1,0:T(8,128)(2,1)} custom-call(f32[80,128]{1,0:T(8,128)S(1)} %add_add_fusion.mine, f32[80,128]{1,0:T(8,128)S(1)} %collective-permute-done.6.theirs, bf16[80,32768]{1,0:T(8,128)(2,1)} %ensemble.1), custom_call_target="tpu_custom_call" | custom-call | tf_op jit(solution)/shard_map/analysis/pallas_call | solution.py:207
  (3 shorter events, 0.0 us)
Async XLA Ops:
  3.6 2.5 %collective-permute-start = (f32[80,128]{1,0:T(8,128)S(1)}, f32[80,128]{1,0:T(8,128)S(1)}, u32[]{:S(2)}, u32[]{:S(2)}) collective-permute-start(f32[80,128]{1,0:T(8,128)S(1)} %get-tuple-element.14), channel_id=1, source_target_pairs={{0,1},{1,0},{2,3},{3,2},{4,5},{5,4},{6,7},{7,6},{8,9},{9,8},{10,11... | collective-permute-start | bytes 122888 | tf_op jit(solution)/shard_map/ppermute | solution.py:243
  6.1 4.5 %collective-permute-start.3 = (f32[80,128]{1,0:T(8,128)S(1)}, f32[80,128]{1,0:T(8,128)S(1)}, u32[]{:S(2)}, u32[]{:S(2)}) collective-permute-start(f32[80,128]{1,0:T(8,128)S(1)} %one_gram.2), channel_id=1, source_target_pairs={{0,1},{1,0},{2,3},{3,2},{4,5},{5,4},{6,7},{7,6},{8,9},{9,8},{10,11... | collective-permute-start | bytes 122888 | tf_op jit(solution)/shard_map/ppermute | solution.py:246
  6.3 10.0 %collective-permute-start.1 = (f32[80,128]{1,0:T(8,128)S(1)}, f32[80,128]{1,0:T(8,128)S(1)}, u32[]{:S(2)}, u32[]{:S(2)}) collective-permute-start(f32[80,128]{1,0:T(8,128)S(1)} %add.22), channel_id=1, source_target_pairs={{0,4},{1,7},{2,6},{3,5},{4,8},{5,11},{6,10},{7,9},{8,12},{9,15},{1... | collective-permute-start | bytes 122888 | tf_op jit(solution)/shard_map/ppermute | solution.py:248
  10.1 6.2 %collective-permute-start.2 = (f32[80,128]{1,0:T(8,128)S(1)}, f32[80,128]{1,0:T(8,128)S(1)}, u32[]{:S(2)}, u32[]{:S(2)}) collective-permute-start(f32[80,128]{1,0:T(8,128)S(1)} %one_gram.3), channel_id=1, source_target_pairs={{0,2},{1,3},{2,0},{3,1},{4,5},{5,4},{6,7},{7,6},{8,9},{9,8},{10,11... | collective-permute-start | bytes 122888 | tf_op jit(solution)/shard_map/ppermute | solution.py:249
  10.5 6.8 %collective-permute-start.4 = (f32[80,128]{1,0:T(8,128)S(1)}, f32[80,128]{1,0:T(8,128)S(1)}, u32[]{:S(2)}, u32[]{:S(2)}) collective-permute-start(f32[80,128]{1,0:T(8,128)S(1)} %add.25), channel_id=1, source_target_pairs={{0,124},{1,127},{2,126},{3,125},{4,0},{5,3},{6,2},{7,1},{8,4},{9,7... | collective-permute-start | bytes 122888 | tf_op jit(solution)/shard_map/ppermute | solution.py:250
  16.3 1.2 %collective-permute-start.5 = (f32[80,128]{1,0:T(8,128)S(1)}, f32[80,128]{1,0:T(8,128)S(1)}, u32[]{:S(2)}, u32[]{:S(2)}) collective-permute-start(f32[80,128]{1,0:T(8,128)S(1)} %one_gram.3), channel_id=1, source_target_pairs={{0,1},{1,0},{2,3},{3,2},{4,6},{5,7},{6,4},{7,5},{8,10},{9,11},{10,... | collective-permute-start | bytes 122888 | tf_op jit(solution)/shard_map/ppermute | solution.py:251
  17.5 1.3 %collective-permute-start.6 = (f32[80,128]{1,0:T(8,128)S(1)}, f32[80,128]{1,0:T(8,128)S(1)}, u32[]{:S(2)}, u32[]{:S(2)}) collective-permute-start(f32[80,128]{1,0:T(8,128)S(1)} %add_add_fusion.mine), channel_id=1, source_target_pairs={{0,1},{1,0},{2,3},{3,2},{4,5},{5,4},{6,7},{7,6},{8,9},{9,8},{10,11... | collective-permute-start | bytes 122888 | tf_op jit(solution)/shard_map/ppermute | solution.py:254

commit v7 on v6

--- a/solution.py
+++ b/solution.py
@@ -234,8 +234,8 @@
     core = pairs(lambda t, l: (t, l ^ 1))
     onward = pairs(lambda t, l: ((t + 1) % n_tile, l ^ (2 * (l & 1))))
     back = pairs(lambda t, l: ((t - 1) % n_tile, l ^ (2 * (l & 1))))
-    early = pairs(lambda t, l: (t, l ^ 2 if t % 8 == 0 else l ^ 1))
-    late = pairs(lambda t, l: (t, l ^ 1 if t % 8 == 0 else l ^ 2))
+    early = pairs(lambda t, l: (t, l ^ 2 if t % 2 == 0 else l ^ 1))
+    late = pairs(lambda t, l: (t, l ^ 1 if t % 2 == 0 else l ^ 2))
     after, right, row_before, row_own = next_gram(
         obs_pert, innovation[None, :], obs_rinv[None, :], loc_weight, obs_count
     )
@@ -249,7 +249,7 @@
     from_early = lax.ppermute(own, axes, early)
     from_after = lax.ppermute(before, axes, back)
     from_late = lax.ppermute(held, axes, late)
-    first = lax.axis_index("tile") % 8 == 0
+    first = lax.axis_index("tile") % 2 == 0
     mine = from_before + jnp.where(first, from_early, 0.0) + from_after + jnp.where(first, 0.0, from_late) + own
     return analysis((mine, lax.ppermute(mine, axes, core)), ensemble)
 

time: 24.8 us -> 24.8 us (level)
  no operation moved by 1% of the time
where the time goes in v7:
time: 24.8 us; the launch traced here: 24.7 us
  starting transfers between devices  11 us (44%)
  Pallas kernels  10.7 us (43%)
  waiting for transfers between devices  2.28 us (9%)
  between operations  0.7 us (3%)
    pallas_call x1, Pallas kernels, analysis(): pl.pallas_call(analysis_kernel, in_specs=[pl.BlockSpec(memory_space=pltpu...  5.86 us
    ppermute x1, starting transfers between devices, local(): from_after = lax.ppermute(before, axes, back)  5.72 us
    pallas_call x1, Pallas kernels, next_gram(): pl.pallas_call(next_kernel, in_specs=[pl.BlockSpec(memory_space=pltpu.SME...  2.9 us
    ppermute x1, starting transfers between devices, local(): from_before = lax.ppermute(after, axes, onward)  2.82 us
    pallas_call x2, Pallas kernels, one_gram(): pl.pallas_call(one_kernel, in_specs=[pl.BlockSpec(memory_space=pltpu.VMEM...  1.91 us
    ppermute x1, starting transfers between devices, local(): after = after + lax.ppermute(after, axes, core)  1.5 us
    ppermute x1, waiting for transfers between devices, local(): from_after = lax.ppermute(before, axes, back)  1.09 us
    ppermute x1, waiting for transfers between devices, local(): return analysis((mine, lax.ppermute(mine, axes, core)), ensemble)  1.06 us
  transfers between devices with their start and end apart: 7, of which 3 were waited for; matrix products, arithmetic and copies ran while one was open for 0% of the time, Pallas kernels for 8%

profile of v7, /device:TPU:1, one launch (start us, length us, event | category | flops | bytes accessed | tf_op | source)
XLA Modules:
  0.0 24.7 jit_solution(2499972161700652743)
XLA Ops:
  0.7 2.9 %next_gram.1 = (f32[80,128]{1,0:T(8,128)S(1)}, bf16[96,16384]{1,0:T(8,128)(2,1)S(1)}, bf16[1,16384]{1,0:T(2,128)(2,1)S(1)}, bf16[1,16384]{1,0:T(2,128)(2,1)S(1)}) custom-call(s32[1]{0:T(128)S(6)} %copy.7.count, bf16[80,16384]{1,0:T(8,128)(2,1)} %pert.1, f32[1,16384]{1,0:T(1,128)} %bitcast.2, f32[1,16384]{1,0:T(1,128)} %bitcast.3, f32[3,16384]{1,0:T(4,128)} %loc.1), custom_call_target="tpu_custom_call" | custom-call | tf_op jit(solution)/shard_map/next_gram/pallas_call | solution.py:76
  3.6 1.5 %collective-permute-start = (f32[80,128]{1,0:T(8,128)S(1)}, f32[80,128]{1,0:T(8,128)S(1)}, u32[]{:S(2)}, u32[]{:S(2)}) collective-permute-start(f32[80,128]{1,0:T(8,128)S(1)} %get-tuple-element.14), channel_id=1, source_target_pairs={{0,1},{1,0},{2,3},{3,2},{4,5},{5,4},{6,7},{7,6},{8,9},{9,8},{10,11... | collective-permute-start | bytes 122888 | tf_op jit(solution)/shard_map/ppermute | solution.py:243
  5.1 1.0 %one_gram.2 = f32[80,128]{1,0:T(8,128)S(1)} custom-call(bf16[96,16384]{1,0:T(8,128)(2,1)S(1)} %get-tuple-element.15.right, bf16[1,16384]{1,0:T(2,128)(2,1)S(1)} %get-tuple-element.16.own), custom_call_target="tpu_custom_call" | custom-call | flops 335544320 | bytes 3145728 | tf_op jit(solution)/shard_map/one_gram/pallas_call | solution.py:106
  6.0 0.0 collective-permute-done
  6.1 0.3 %collective-permute-start.3 = (f32[80,128]{1,0:T(8,128)S(1)}, f32[80,128]{1,0:T(8,128)S(1)}, u32[]{:S(2)}, u32[]{:S(2)}) collective-permute-start(f32[80,128]{1,0:T(8,128)S(1)} %one_gram.2), channel_id=1, source_target_pairs={{0,1},{1,0},{2,3},{3,2},{4,5},{5,4},{6,7},{7,6},{8,9},{9,8},{10,11... | collective-permute-start | bytes 122888 | tf_op jit(solution)/shard_map/ppermute | solution.py:246
  6.3 2.8 %collective-permute-start.1 = (f32[80,128]{1,0:T(8,128)S(1)}, f32[80,128]{1,0:T(8,128)S(1)}, u32[]{:S(2)}, u32[]{:S(2)}) collective-permute-start(f32[80,128]{1,0:T(8,128)S(1)} %add.22), channel_id=1, source_target_pairs={{0,4},{1,7},{2,6},{3,5},{4,8},{5,11},{6,10},{7,9},{8,12},{9,15},{1... | collective-permute-start | bytes 122888 | tf_op jit(solution)/shard_map/ppermute | solution.py:248
  9.1 1.0 %one_gram.3 = f32[80,128]{1,0:T(8,128)S(1)} custom-call(bf16[96,16384]{1,0:T(8,128)(2,1)S(1)} %get-tuple-element.15.right, bf16[1,16384]{1,0:T(2,128)(2,1)S(1)} %get-tuple-element.19.own), custom_call_target="tpu_custom_call" | custom-call | flops 335544320 | bytes 3145728 | tf_op jit(solution)/shard_map/one_gram/pallas_call | solution.py:106
  10.1 0.4 %collective-permute-start.2 = (f32[80,128]{1,0:T(8,128)S(1)}, f32[80,128]{1,0:T(8,128)S(1)}, u32[]{:S(2)}, u32[]{:S(2)}) collective-permute-start(f32[80,128]{1,0:T(8,128)S(1)} %one_gram.3), channel_id=1, source_target_pairs={{0,2},{1,3},{2,0},{3,1},{4,5},{5,4},{6,7},{7,6},{8,10},{9,11},{10,... | collective-permute-start | bytes 122888 | tf_op jit(solution)/shard_map/ppermute | solution.py:249
  10.5 0.0 collective-permute-done.3
  10.5 5.7 %collective-permute-start.4 = (f32[80,128]{1,0:T(8,128)S(1)}, f32[80,128]{1,0:T(8,128)S(1)}, u32[]{:S(2)}, u32[]{:S(2)}) collective-permute-start(f32[80,128]{1,0:T(8,128)S(1)} %add.25), channel_id=1, source_target_pairs={{0,124},{1,127},{2,126},{3,125},{4,0},{5,3},{6,2},{7,1},{8,4},{9,7... | collective-permute-start | bytes 122888 | tf_op jit(solution)/shard_map/ppermute | solution.py:250
  16.3 0.0 collective-permute-start.5
  16.3 0.0 collective-permute-done.1
  16.3 0.0 collective-permute-done.2
  16.3 1.1 %collective-permute-done.4 = f32[80,128]{1,0:T(8,128)S(1)} collective-permute-done((f32[80,128]{1,0:T(8,128)S(1)}, f32[80,128]{1,0:T(8,128)S(1)}, u32[]{:S(2)}, u32[]{:S(2)}) %collective-permute-start.4) | collective-permute-done | bytes 40992 | tf_op jit(solution)/shard_map/ppermute | solution.py:250
  17.4 0.1 collective-permute-done.5
  17.5 0.2 collective-permute-start.6
  17.7 1.1 %collective-permute-done.6.theirs = f32[80,128]{1,0:T(8,128)S(1)} collective-permute-done((f32[80,128]{1,0:T(8,128)S(1)}, f32[80,128]{1,0:T(8,128)S(1)}, u32[]{:S(2)}, u32[]{:S(2)}) %collective-permute-start.6) | collective-permute-done | bytes 40992 | tf_op jit(solution)/shard_map/ppermute | solution.py:254
  18.8 5.9 %analysis.1 = bf16[80,32768]{1,0:T(8,128)(2,1)} custom-call(f32[80,128]{1,0:T(8,128)S(1)} %add_add_fusion.mine, f32[80,128]{1,0:T(8,128)S(1)} %collective-permute-done.6.theirs, bf16[80,32768]{1,0:T(8,128)(2,1)} %ensemble.1), custom_call_target="tpu_custom_call" | custom-call | tf_op jit(solution)/shard_map/analysis/pallas_call | solution.py:207
  (3 shorter events, 0.0 us)
Async XLA Ops:
  3.6 2.5 %collective-permute-start = (f32[80,128]{1,0:T(8,128)S(1)}, f32[80,128]{1,0:T(8,128)S(1)}, u32[]{:S(2)}, u32[]{:S(2)}) collective-permute-start(f32[80,128]{1,0:T(8,128)S(1)} %get-tuple-element.14), channel_id=1, source_target_pairs={{0,1},{1,0},{2,3},{3,2},{4,5},{5,4},{6,7},{7,6},{8,9},{9,8},{10,11... | collective-permute-start | bytes 122888 | tf_op jit(solution)/shard_map/ppermute | solution.py:243
  6.1 4.5 %collective-permute-start.3 = (f32[80,128]{1,0:T(8,128)S(1)}, f32[80,128]{1,0:T(8,128)S(1)}, u32[]{:S(2)}, u32[]{:S(2)}) collective-permute-start(f32[80,128]{1,0:T(8,128)S(1)} %one_gram.2), channel_id=1, source_target_pairs={{0,1},{1,0},{2,3},{3,2},{4,5},{5,4},{6,7},{7,6},{8,9},{9,8},{10,11... | collective-permute-start | bytes 122888 | tf_op jit(solution)/shard_map/ppermute | solution.py:246
  6.3 10.0 %collective-permute-start.1 = (f32[80,128]{1,0:T(8,128)S(1)}, f32[80,128]{1,0:T(8,128)S(1)}, u32[]{:S(2)}, u32[]{:S(2)}) collective-permute-start(f32[80,128]{1,0:T(8,128)S(1)} %add.22), channel_id=1, source_target_pairs={{0,4},{1,7},{2,6},{3,5},{4,8},{5,11},{6,10},{7,9},{8,12},{9,15},{1... | collective-permute-start | bytes 122888 | tf_op jit(solution)/shard_map/ppermute | solution.py:248
  10.1 6.2 %collective-permute-start.2 = (f32[80,128]{1,0:T(8,128)S(1)}, f32[80,128]{1,0:T(8,128)S(1)}, u32[]{:S(2)}, u32[]{:S(2)}) collective-permute-start(f32[80,128]{1,0:T(8,128)S(1)} %one_gram.3), channel_id=1, source_target_pairs={{0,2},{1,3},{2,0},{3,1},{4,5},{5,4},{6,7},{7,6},{8,10},{9,11},{10,... | collective-permute-start | bytes 122888 | tf_op jit(solution)/shard_map/ppermute | solution.py:249
  10.5 6.8 %collective-permute-start.4 = (f32[80,128]{1,0:T(8,128)S(1)}, f32[80,128]{1,0:T(8,128)S(1)}, u32[]{:S(2)}, u32[]{:S(2)}) collective-permute-start(f32[80,128]{1,0:T(8,128)S(1)} %add.25), channel_id=1, source_target_pairs={{0,124},{1,127},{2,126},{3,125},{4,0},{5,3},{6,2},{7,1},{8,4},{9,7... | collective-permute-start | bytes 122888 | tf_op jit(solution)/shard_map/ppermute | solution.py:250
  16.3 1.2 %collective-permute-start.5 = (f32[80,128]{1,0:T(8,128)S(1)}, f32[80,128]{1,0:T(8,128)S(1)}, u32[]{:S(2)}, u32[]{:S(2)}) collective-permute-start(f32[80,128]{1,0:T(8,128)S(1)} %one_gram.3), channel_id=1, source_target_pairs={{0,1},{1,0},{2,3},{3,2},{4,6},{5,7},{6,4},{7,5},{8,9},{9,8},{10,11... | collective-permute-start | bytes 122888 | tf_op jit(solution)/shard_map/ppermute | solution.py:251
  17.5 1.3 %collective-permute-start.6 = (f32[80,128]{1,0:T(8,128)S(1)}, f32[80,128]{1,0:T(8,128)S(1)}, u32[]{:S(2)}, u32[]{:S(2)}) collective-permute-start(f32[80,128]{1,0:T(8,128)S(1)} %add_add_fusion.mine), channel_id=1, source_target_pairs={{0,1},{1,0},{2,3},{3,2},{4,5},{5,4},{6,7},{7,6},{8,9},{9,8},{10,11... | collective-permute-start | bytes 122888 | tf_op jit(solution)/shard_map/ppermute | solution.py:254
